TPU v7x, 512 devices: a whole 4x8x8 slice. The times are simulated.
512 devices in a mesh: dom: 64 (over z, x, core), feat: 8 (over y).
Axes of the slice: x: 4, y: 8, z: 8, core: 2. Of those that a mesh axis runs over, the one named last changes fastest.
Arguments:
- features: bfloat16 [128, 131072], P('feat', 'dom'), may hold values from -6 to 6
- self_weight: bfloat16 [128, 256], replicated, may hold values from -0.5 to 0.5
- neigh_weight: bfloat16 [128, 256], replicated, may hold values from -0.5 to 0.5
- bias_vector: float32 [256], replicated, may hold values from -3 to 3
- tile_values: bfloat16 [4096, 128, 128], P('dom'), may hold values from -0.625 to 0.625
- tile_rows: int32 [4096], P('dom'), may hold values from 0 to 15
- tile_cols: int32 [4096], P('dom'), may hold values from 0 to 271, as said below
- send_blocks: int32 [64, 64, 4], P('dom'), may hold values from -1 to 15, as said below
- cotangent: bfloat16 [256, 131072], P('feat', 'dom'), may hold values from -6 to 6
Outputs:
- activated: bfloat16 [256, 131072], P('feat', 'dom')
- grad_features: bfloat16 [128, 131072], P('feat', 'dom')
- grad_self: float32 [128, 256], replicated
- grad_neigh: float32 [128, 256], replicated
- grad_bias: float32 [256], replicated
Inputs may be any that keep to these rules, and one draw needn't show every extreme that they name: `send_blocks`: entry [s, d, c] is the local block (0 to 15) that partition s sends to partition d in slot c, or -1 for an empty slot. Only d = s + 1, s + 2, s - 1 and s + 64 / 2 (modulo 64) have live slots; live slots come first. Partition 0 sends 4 blocks to each of its four neighbours and receives 4 from each. `tile_cols`: values under 16 name a local column block; 16 + s * 4 + c names the block that partition s sends to this partition in slot c, which is always a live slot. Every live slot is named by some tile.
All inputs are finite; a program needn't handle non-finite values.
Results may differ from a plain program's by a relative error of at most 0.009.
Values may be sent and summed in bfloat16 or wider, within the bound.
A program may use at most 64 MiB of HBM per device.

v0:
```python
import math

import jax
import jax.numpy as jnp
from jax import lax
from jax.sharding import PartitionSpec as P


def local(
    features,
    self_weight,
    neigh_weight,
    bias_vector,
    tile_values,
    tile_rows,
    tile_cols,
    send_blocks,
    cotangent,
):
    feat_rows, vertex_count = features.shape
    block_size = tile_values.shape[1]
    block_count = vertex_count // block_size
    dom_size = lax.axis_size("dom")
    feat_size = lax.axis_size("feat")
    feat_index = lax.axis_index("feat")
    slot_count = send_blocks.shape[2]
    hidden_dim = self_weight.shape[1]
    in_dim = self_weight.shape[0]
    hidden_rows = hidden_dim // feat_size
    local_blocks = features.reshape(feat_rows, block_count, block_size).transpose(1, 0, 2)
    send_table = send_blocks[0]
    safe_index = jnp.clip(send_table, 0, block_count - 1)
    live_slots = send_table >= 0
    outgoing = jnp.where(
        live_slots[:, :, None, None], local_blocks[safe_index], jnp.zeros((), jnp.bfloat16)
    )
    incoming = lax.all_to_all(outgoing, "dom", split_axis=0, concat_axis=0, tiled=True)
    received = incoming.reshape(dom_size * slot_count, feat_rows, block_size)
    table = jnp.concatenate([local_blocks, received], axis=0)
    table_size = table.shape[0]
    gathered = table[tile_cols]
    products = jnp.einsum("tfk,tjk->tfj", gathered, tile_values, preferred_element_type=jnp.float32)
    agg_blocks = (
        jnp.zeros((block_count, feat_rows, block_size), jnp.float32).at[tile_rows].add(products)
    )
    agg = agg_blocks.transpose(1, 0, 2).reshape(feat_rows, vertex_count).astype(jnp.bfloat16)
    self_rows = lax.dynamic_slice_in_dim(self_weight, feat_index * feat_rows, feat_rows, 0)
    neigh_rows = lax.dynamic_slice_in_dim(neigh_weight, feat_index * feat_rows, feat_rows, 0)
    bias_part = lax.dynamic_slice_in_dim(bias_vector, feat_index * hidden_rows, hidden_rows, 0)
    term = jnp.einsum("fh,fv->hv", self_rows, features, preferred_element_type=jnp.float32)
    pre = (
        lax.psum_scatter(
            term + jnp.einsum("fh,fv->hv", neigh_rows, agg, preferred_element_type=jnp.float32),
            "feat",
            scatter_dimension=0,
            tiled=True,
        )
        + bias_part[:, None]
    )
    sigma = jax.nn.sigmoid(pre)
    activated = (pre * sigma).astype(jnp.bfloat16)
    dpre = (cotangent.astype(jnp.float32) * sigma * (1.0 + pre * (1.0 - sigma))).astype(
        jnp.bfloat16
    )
    full_dpre = lax.all_gather(dpre, "feat", axis=0, tiled=True)
    back_self = jnp.einsum(
        "fh,hv->fv", self_rows, full_dpre, preferred_element_type=jnp.float32
    ).astype(jnp.bfloat16)
    back_neigh = jnp.einsum(
        "fh,hv->fv", neigh_rows, full_dpre, preferred_element_type=jnp.float32
    ).astype(jnp.bfloat16)
    self_slab = jnp.einsum("fv,hv->fh", features, full_dpre, preferred_element_type=jnp.float32)
    neigh_slab = jnp.einsum("fv,hv->fh", agg, full_dpre, preferred_element_type=jnp.float32)
    empty_grad = jnp.zeros((in_dim, hidden_dim), jnp.float32)
    part_self = lax.dynamic_update_slice(empty_grad, self_slab, (feat_index * feat_rows, 0))
    part_neigh = lax.dynamic_update_slice(empty_grad, neigh_slab, (feat_index * feat_rows, 0))
    bias_slab = jnp.sum(dpre.astype(jnp.float32), axis=1)
    part_bias = lax.dynamic_update_slice(
        jnp.zeros((hidden_dim,), jnp.float32), bias_slab, (feat_index * hidden_rows,)
    )
    summed_self, summed_neigh, summed_bias = lax.psum(
        (part_self, part_neigh, part_bias), ("dom", "feat")
    )
    norm_scale = 1.0 / math.sqrt(vertex_count * dom_size)
    grad_self = summed_self * norm_scale
    grad_neigh = summed_neigh * norm_scale
    grad_bias = summed_bias * norm_scale
    neigh_blocks = back_neigh.reshape(feat_rows, block_count, block_size).transpose(1, 0, 2)
    selected = neigh_blocks[tile_rows]
    contrib = jnp.einsum("tfj,tjk->tfk", selected, tile_values, preferred_element_type=jnp.float32)
    spread_blocks = (
        jnp.zeros((table_size, feat_rows, block_size), jnp.float32).at[tile_cols].add(contrib)
    )
    local_part = spread_blocks[:block_count]
    returned = spread_blocks[block_count:]
    back_terms = lax.all_to_all(
        returned.reshape(dom_size, slot_count, feat_rows, block_size),
        "dom",
        split_axis=0,
        concat_axis=0,
        tiled=True,
    )
    flat_terms = back_terms.reshape(dom_size * slot_count, feat_rows, block_size)
    owners = send_table.reshape(dom_size * slot_count)
    owner_index = jnp.where(owners >= 0, owners, block_count)
    from_peers = (
        jnp.zeros((block_count, feat_rows, block_size), jnp.float32)
        .at[owner_index]
        .add(flat_terms, mode="drop")
    )
    graph_term = (local_part + from_peers).transpose(1, 0, 2).reshape(feat_rows, vertex_count)
    grad_features = (back_self.astype(jnp.float32) + graph_term).astype(jnp.bfloat16)
    return (activated, grad_features, grad_self, grad_neigh, grad_bias)


def solution(mesh):
    in_specs = (
        P("feat", "dom"),
        P(),
        P(),
        P(),
        P("dom", None, None),
        P("dom"),
        P("dom"),
        P("dom", None, None),
        P("feat", "dom"),
    )
    out_specs = (P("feat", "dom"), P("feat", "dom"), P(), P(), P())
    return jax.shard_map(local, mesh=mesh, in_specs=in_specs, out_specs=out_specs, check_vma=False)
```

profile of v0, /device:TPU:1, one launch (start us, length us, event | category | flops | bytes accessed | tf_op | source)
XLA Modules:
  0.0 608.7 jit_solution(5821506732936640660)
XLA Ops:
  7.2 0.8 compare_select_fusion.2
  8.0 0.7 compare_bitcast_fusion
  8.7 0.9 bitcast_bitcast_fusion.1
  9.9 0.8 gather_fusion
  10.8 1.3 broadcast_select_fusion
  12.0 14.8 %all-to-all-start = ((bf16[64,4,16,128]{3,2,1,0:T(8,128)(2,1)}), bf16[64,4,16,128]{3,2,1,0:T(8,128)(2,1)S(1)}, u32[]{:S(2)}, u32[]{:S(2)}) async-start(bf16[64,4,16,128]{3,2,1,0:T(8,128)(2,1)} %broadcast_select_fusion), calls=%async_computation | async-start | bytes 2097152 | tf_op jit(solution)/shard_map/all_to_all | solution.py:37
  27.0 2.5 fusion.12
  29.5 25.4 %all-to-all-done = bf16[64,4,16,128]{3,2,1,0:T(8,128)(2,1)S(1)} async-done(((bf16[64,4,16,128]{3,2,1,0:T(8,128)(2,1)}), bf16[64,4,16,128]{3,2,1,0:T(8,128)(2,1)S(1)}, u32[]{:S(2)}, u32[]{:S(2)}) %all-to-all-start) | async-done | bytes 1048608 | tf_op jit(solution)/shard_map/all_to_all | solution.py:37
  54.9 1.1 pad_maximum_fusion
  56.0 1.9 gather_fusion.1
  57.9 1.2 fusion.18
  59.1 2.9 scatter_fusion
  62.0 3.4 convolution_add_fusion
  65.5 0.6 copy-done.7
  66.2 37.0 %reduce-scatter.2.cloned.1.call-done = f32[32,2048]{1,0:T(8,128)} async-done(((f32[256,2048]{1,0:T(8,128)}), f32[32,2048]{1,0:T(8,128)}) %reduce-scatter.2.cloned.1.call-update) | async-done | bytes 262160 | tf_op jit(solution)/shard_map/reduce_scatter | solution.py:52
  103.2 2.0 convert_reduce_fusion
  105.2 40.1 %all-gather.2.cloned.1.call-done = bf16[256,2048]{1,0:T(8,128)(2,1)} async-done(((bf16[32,2048]{1,0:T(8,128)(2,1)}), bf16[256,2048]{1,0:T(8,128)(2,1)}) %all-gather.2.cloned.1.call-update) | async-done | bytes 1048592 | tf_op jit(solution)/shard_map/all_gather | solution.py:65
  145.3 1.5 fusion.3
  146.8 0.6 gather_fusion.2
  147.4 0.7 fusion.19
  148.1 1.5 broadcast_in_dim.41
  149.6 7.5 %scatter_fusion.1 = f32[272,16,128]{2,1,0:T(8,128)} fusion(f32[272,16,128]{2,1,0:T(8,128)} %broadcast_in_dim.41, s32[64]{0:T(128)S(1)} %compare_select_fusion.3, f32[64,16,128]{2,1,0:T(8,128)S(1)} %fusion.19), kind=kCustom, calls=%fused_computation.4 | custom fusion | flops 131072 | bytes 1573120 | tf_op jit(solution)/shard_map/scatter-add | solution.py:92
  157.1 3.1 slice.15
  160.2 16.1 %all-to-all-start.1 = ((f32[64,4,16,128]{3,2,1,0:T(8,128)}), f32[64,4,16,128]{3,2,1,0:T(8,128)}, u32[]{:S(2)}, u32[]{:S(2)}) async-start(f32[64,4,16,128]{3,2,1,0:T(8,128)} %bitcast.58), calls=%async_computation.2 | async-start | bytes 4194304 | tf_op jit(solution)/shard_map/all_to_all | solution.py:96
  176.8 134.8 %psum.23 = f32[256]{0:T(256)S(1)} all-reduce(f32[256]{0:T(256)S(1)} %dynamic_update_slice.11), channel_id=1, replica_groups=mesh['dom'=64,'feat'=8] {'dom','feat'}, use_global_device_ids=true, to_apply=%region_7.8 | all-reduce | flops 256 | bytes 2048 | tf_op jit(solution)/shard_map/psum | solution.py:81
  312.7 0.4 copy-done.3
  313.2 0.6 broadcast_multiply_fusion.2
  313.7 0.9 slice.14
  314.6 263.4 %all-reduce.3.cloned.1.call-done = (f32[128,256]{1,0:T(8,128)}, f32[128,256]{1,0:T(8,128)}) async-done(((f32[128,256]{1,0:T(8,128)}, f32[128,256]{1,0:T(8,128)}), (f32[128,256]{1,0:T(8,128)}, f32[128,256]{1,0:T(8,128)})) %all-reduce.3.cloned.1.call-update) | async-done | bytes 262160 | tf_op jit(solution)/shard_map/psum | solution.py:81
  578.0 1.7 broadcast_multiply_fusion
  579.7 20.8 %scatter_fusion.2 = f32[16,16,128]{2,1,0:T(8,128)S(1)} fusion(f32[16,16,128]{2,1,0:T(8,128)S(1)} %slice.14, s32[256]{0:T(256)S(1)} %bitcast.62, f32[256,16,128]{2,1,0:T(8,128)} %bitcast.9), kind=kCustom, calls=%fused_computation.5 | custom fusion | flops 524288 | bytes 6292480 | tf_op jit(solution)/shard_map/scatter-add | solution.py:109
  600.6 1.6 fusion.2
  (45 shorter events, 2.2 us)
Async XLA Ops:
  7.2 50.7 %copy-start = (bf16[64,128,128]{2,1,0:T(8,128)(2,1)S(1)}, bf16[64,128,128]{2,1,0:T(8,128)(2,1)}, u32[]{:S(2)}) copy-start(bf16[64,128,128]{2,1,0:T(8,128)(2,1)} %param.13) | copy-start | bytes 6291460
  10.7 16.2 %copy-start.8 = (s32[64]{0:T(128)S(1)}, s32[64]{0:T(128)}, u32[]{:S(2)}) copy-start(s32[64]{0:T(128)} %param.15) | copy-start | bytes 772
  10.7 16.2 %copy-start.9 = (s32[64]{0:T(128)S(1)}, s32[64]{0:T(128)}, u32[]{:S(2)}) copy-start(s32[64]{0:T(128)} %param.14) | copy-start | bytes 772
  10.8 16.2 %copy-start.2 = (bf16[16,2048]{1,0:T(8,128)(2,1)S(1)}, bf16[16,2048]{1,0:T(8,128)(2,1)}, u32[]{:S(2)}) copy-start(bf16[16,2048]{1,0:T(8,128)(2,1)} %param.9) | copy-start | bytes 196612
  12.0 42.8 %all-to-all-start = ((bf16[64,4,16,128]{3,2,1,0:T(8,128)(2,1)}), bf16[64,4,16,128]{3,2,1,0:T(8,128)(2,1)S(1)}, u32[]{:S(2)}, u32[]{:S(2)}) async-start(bf16[64,4,16,128]{3,2,1,0:T(8,128)(2,1)} %broadcast_select_fusion), calls=%async_computation | async-start | bytes 2097152 | tf_op jit(solution)/shard_map/all_to_all | solution.py:37
  26.9 76.3 %reduce-scatter.2.cloned.1.call-start = ((), (), s32[]{:S(2)}) async-start(), calls=%async_computation.3 | async-start | bytes 2359296 | tf_op jit(solution)/shard_map/reduce_scatter | solution.py:52
  65.4 0.7 copy-start.7
  65.4 37.7 %copy-start.5 = (bf16[32,2048]{1,0:T(8,128)(2,1)S(1)}, bf16[32,2048]{1,0:T(8,128)(2,1)}, u32[]{:S(2)}) copy-start(bf16[32,2048]{1,0:T(8,128)(2,1)} %param.17) | copy-start | bytes 393220
  65.5 79.8 %all-gather.2.cloned.1.call-start = ((), (), s32[]{:S(2)}) async-start(), calls=%async_computation.4 | async-start | bytes 1179648 | tf_op jit(solution)/shard_map/all_gather | solution.py:65
  160.2 16.1 %copy-start.6 = (s32[1,64,4]{1,2,0:T(4,128)S(1)}, s32[1,64,4]{1,2,0:T(4,128)}, u32[]{:S(2)}) copy-start(s32[1,64,4]{1,2,0:T(4,128)} %param.16) | copy-start | bytes 3076
  160.2 151.5 %copy-start.1 = (bf16[256,2048]{1,0:T(8,128)(2,1)S(1)}, bf16[256,2048]{1,0:T(8,128)(2,1)}, u32[]{:S(2)}) copy-start(bf16[256,2048]{1,0:T(8,128)(2,1)} %all-gather.2.cloned.1.call-done) | copy-start | bytes 3145732
  160.2 419.5 %all-to-all-start.1 = ((f32[64,4,16,128]{3,2,1,0:T(8,128)}), f32[64,4,16,128]{3,2,1,0:T(8,128)}, u32[]{:S(2)}, u32[]{:S(2)}) async-start(f32[64,4,16,128]{3,2,1,0:T(8,128)} %bitcast.58), calls=%async_computation.2 | async-start | bytes 4194304 | tf_op jit(solution)/shard_map/all_to_all | solution.py:96
  176.3 401.7 %all-reduce.3.cloned.1.call-start = ((), (), s32[]{:S(2)}) async-start(), calls=%async_computation.5 | async-start | bytes 524288 | tf_op jit(solution)/shard_map/psum | solution.py:81
  312.0 0.7 copy-start.4
  312.5 0.7 copy-start.3
Sparse Core Ops, SparseCore 0:
  65.6 37.5 reduce-scatter.1
  105.8 39.4 all-gather.1
  313.3 264.7 all-reduce.2
where the time goes:
time: 610 us; the launch traced here: 609 us
  waiting for transfers between devices  366 us (60%)
  blocking collectives  135 us (22%)
  other arithmetic  39.4 us (6%)
  starting transfers between devices  31 us (5%)
  between operations  14 us (2%)
  local copies, waits for them, and re-layouts  11.9 us (2%)
  matrix products  11.6 us (2%)
    psum x1, waiting for transfers between devices, local(): lax.psum((part_self, part_neigh, part_bias), ('dom', 'feat'))  263 us
    psum x1, blocking collectives, local(): lax.psum((part_self, part_neigh, part_bias), ('dom', 'feat'))  135 us
    all_gather x1, waiting for transfers between devices, local(): full_dpre = lax.all_gather(dpre, 'feat', axis=0, tiled=True)  40.1 us
    reduce_scatter x1, waiting for transfers between devices, local(): lax.psum_scatter(term + jnp.einsum('fh,fv->hv', neigh_rows, agg, preferre...  37 us
    all_to_all x1, waiting for transfers between devices, local(): lax.all_to_all(outgoing, 'dom', split_axis=0, concat_axis=0, tiled=True)  25.4 us
    scatter-add x1, other arithmetic, local(): from_peers = jnp.zeros((block_count, feat_rows, block_size), jnp.float32)...  20.8 us
    all_to_all x1, starting transfers between devices, local(): lax.all_to_all(returned.reshape(dom_size, slot_count, feat_rows, block_si...  16.1 us
    all_to_all x1, starting transfers between devices, local(): lax.all_to_all(outgoing, 'dom', split_axis=0, concat_axis=0, tiled=True)  14.8 us
  transfers between devices with their start and end apart: 5, of which 4 were waited for; matrix products, arithmetic and copies ran while one was open for 1% of the time, Pallas kernels for 0%

commit v1 on v0

v1 whole, which is shorter than its diff:
```python
import functools
import math

import jax
import jax.numpy as jnp
from jax import lax
from jax.experimental import pallas as pl
from jax.experimental.pallas import tpu as pltpu
from jax.sharding import PartitionSpec as P

X_SIZE = 4
CORES = 2
BLOCK = 128
MESH = pl.DeviceIdType.MESH
F32 = jnp.float32
BF16 = jnp.bfloat16


def remote(src, dst, send_sem, recv_sem, device):
    return pltpu.make_async_remote_copy(
        src_ref=src,
        dst_ref=dst,
        send_sem=send_sem,
        recv_sem=recv_sem,
        device_id=device,
        device_id_type=MESH,
    )


def dot_nt(a, b):
    return lax.dot_general(a, b, (((1,), (1,)), ((), ())), preferred_element_type=F32)


def dot_nn(a, b):
    return lax.dot_general(a, b, (((1,), (0,)), ((), ())), preferred_element_type=F32)


def kernel(
    dims,
    tile_rows,
    tile_cols,
    send_blocks,
    features,
    self_weight,
    neigh_weight,
    bias,
    tile_values,
    cotangent,
    activated,
    grad_features,
    grad_self,
    grad_neigh,
    grad_bias,
    slots,
    fv,
    tiles,
    w_self,
    w_neigh,
    w_cat,
    w_t,
    bias_row,
    bias_mat,
    xg,
    ct,
    own_tab,
    tab,
    stage,
    agg,
    act,
    bk,
    bkr,
    btab,
    prod,
    rb_send,
    rb_recv,
    part,
    part_recv,
    rs_src,
    rs_recv,
    y_src,
    y_recv,
    g_full,
    b_full,
    local_sem,
    own_sem,
    halo_sem,
    feat_sem,
    cot_sem,
    agg_sem,
    back_sem,
    act_sem,
    ret_sem,
    core_sem,
    rs_sem,
    yr_sem,
    ag_sem,
):
    dom_size, y_size, nb, tile_count, in_dim, hidden, norm_scale = dims
    z_size = dom_size // (X_SIZE * CORES)
    xz = X_SIZE * z_size
    fr = in_dim // y_size
    hr = hidden // y_size
    vb = nb // y_size
    vc = vb * BLOCK
    tpq = (in_dim // 8) * (hidden // 128) // xz

    dom = lax.axis_index("dom")
    fy = lax.axis_index("feat")
    core = lax.rem(dom, CORES)
    q = dom // CORES
    my_z = q // X_SIZE
    my_x = lax.rem(q, X_SIZE)

    offsets = (1, 2, dom_size - 1, dom_size // 2)
    y_peers = [lax.rem(fy + i, y_size) for i in range(1, y_size)]
    sibling = (q * CORES + 1 - core, fy)
    xz_peers = []
    for dz in range(z_size):
        for dx in range(X_SIZE):
            if dz or dx:
                pz = lax.rem(my_z + dz, z_size)
                px = lax.rem(my_x + dx, X_SIZE)
                xz_peers.append(pz * X_SIZE + px)

    loads = [
        pltpu.make_async_copy(features, fv, local_sem.at[0]),
        pltpu.make_async_copy(self_weight, w_self, local_sem.at[1]),
        pltpu.make_async_copy(neigh_weight, w_neigh, local_sem.at[2]),
        pltpu.make_async_copy(bias, bias_row, local_sem.at[3]),
        pltpu.make_async_copy(tile_values, tiles, local_sem.at[4]),
    ]
    for copy in loads:
        copy.start()

    barrier = pltpu.get_barrier_semaphore()
    greeted = 0
    for p in y_peers:
        pl.semaphore_signal(barrier, inc=1, device_id=(dom, p), device_id_type=MESH)
        greeted += 1
    for off in (1, 2, dom_size - 1, dom_size - 2, dom_size // 2):
        pl.semaphore_signal(
            barrier, inc=1, device_id=(lax.rem(dom + off, dom_size), fy), device_id_type=MESH
        )
        greeted += 1
    pl.semaphore_signal(barrier, inc=1, device_id=sibling, device_id_type=MESH)
    greeted += 1
    for p in xz_peers:
        pl.semaphore_signal(
            barrier, inc=1, device_id=(p * CORES + core, fy), device_id_type=MESH
        )
        greeted += 1

    def slot_body(t, carry):
        col = tile_cols[t]
        far = jnp.maximum(col - nb, 0)
        back = lax.rem(dom + dom_size - far // 4, dom_size)
        place = jnp.where(
            back == offsets[0],
            0,
            jnp.where(back == offsets[1], 1, jnp.where(back == offsets[2], 2, 3)),
        )
        slots[t] = jnp.where(col < nb, col, nb + place * 4 + lax.rem(far, 4))
        return carry

    lax.fori_loop(0, tile_count, slot_body, 0)

    owners = []
    for pos in range(4):
        to = lax.rem(dom + offsets[pos], dom_size)
        owners.append([send_blocks[0, to, c] for c in range(4)])
    loads[0].wait()
    for b in range(nb):
        own_tab[b] = fv[:, b * BLOCK : (b + 1) * BLOCK]
        tab[b] = fv[:, b * BLOCK : (b + 1) * BLOCK]
    for pos in range(4):
        for c in range(4):
            stage[pos, c] = own_tab[jnp.maximum(owners[pos][c], 0)]

    pl.semaphore_wait(barrier, greeted)

    sends = []
    halo = []
    for pos in range(4):
        to = lax.rem(dom + offsets[pos], dom_size)
        halo.append(
            remote(
                stage.at[pos],
                tab.at[pl.ds(nb + 4 * pos, 4)],
                halo_sem.at[0, pos],
                halo_sem.at[1, pos],
                (to, fy),
            )
        )
        halo[-1].start()
    sends += halo
    feat_in = []
    for i, p in enumerate(y_peers):
        feat_in.append(
            remote(
                fv.at[:, pl.ds(pl.multiple_of(p * vc, vc), vc)],
                xg.at[fy, 0],
                feat_sem.at[0, i],
                feat_sem.at[1, i],
                (dom, p),
            )
        )
        feat_in[-1].start()
    sends += feat_in
    cot_in = []
    for i, p in enumerate(y_peers):
        cot_in.append(
            remote(
                cotangent.at[:, pl.ds(pl.multiple_of(p * vc, vc), vc)],
                ct.at[fy],
                cot_sem.at[0, i],
                cot_sem.at[1, i],
                (dom, p),
            )
        )
        cot_in[-1].start()
    sends += cot_in
    own_feat = pltpu.make_async_copy(
        fv.at[:, pl.ds(pl.multiple_of(fy * vc, vc), vc)], xg.at[fy, 0], own_sem.at[0]
    )
    own_feat.start()
    own_cot = pltpu.make_async_copy(
        cotangent.at[:, pl.ds(pl.multiple_of(fy * vc, vc), vc)], ct.at[fy], own_sem.at[1]
    )
    own_cot.start()

    for copy in loads[1:4]:
        copy.wait()
    for y in range(y_size):
        w_cat[y, 0] = w_self[y * fr : (y + 1) * fr, :]
        w_cat[y, 1] = w_neigh[y * fr : (y + 1) * fr, :]
    weights = w_cat[...].reshape(2 * in_dim, hidden)
    w_t[...] = weights.astype(F32).T.astype(BF16)
    bias_mat[...] = jnp.broadcast_to(bias_row[...], (128, hidden)).T
    loads[4].wait()

    for copy in halo:
        copy.wait_recv()

    zero = jnp.zeros((fr, BLOCK), F32)

    def agg_body(t, sums):
        p = dot_nt(tab[slots[t]], tiles[t])
        r = tile_rows[t]
        return tuple(jnp.where(r == b, s + p, s) for b, s in enumerate(sums))

    sums = lax.fori_loop(0, tile_count, agg_body, (zero,) * nb, unroll=8)
    for b in range(nb):
        agg[b // vb, :, (b % vb) * BLOCK : (b % vb + 1) * BLOCK] = sums[b].astype(BF16)

    agg_in = []
    for i, p in enumerate(y_peers):
        agg_in.append(
            remote(agg.at[p], xg.at[fy, 1], agg_sem.at[0, i], agg_sem.at[1, i], (dom, p))
        )
        agg_in[-1].start()
    sends += agg_in
    xg[fy, 1] = agg[fy]

    own_feat.wait()
    own_cot.wait()
    for copy in feat_in + cot_in + agg_in:
        copy.wait_recv()

    both = xg[...].reshape(2 * in_dim, vc)
    pre = dot_nn(w_t[...], both) + jnp.concatenate([bias_mat[...]] * vb, axis=1)
    sigma = jax.nn.sigmoid(pre)
    cot = ct[...].reshape(hidden, vc).astype(F32)
    dpre = (cot * sigma * (1.0 + pre * (1.0 - sigma))).astype(BF16)
    act[...] = (pre * sigma).astype(BF16).reshape(y_size, hr, vc)
    bk[...] = dot_nn(weights, dpre).astype(BF16).reshape(y_size, 2 * fr, vc)

    back_in = []
    for i, p in enumerate(y_peers):
        back_in.append(
            remote(bk.at[p], bkr.at[fy], back_sem.at[0, i], back_sem.at[1, i], (dom, p))
        )
        back_in[-1].start()
    sends += back_in
    bkr[fy] = bk[fy]

    grads = dot_nt(both, dpre)
    ones = jnp.ones((16, vc), BF16)
    bias_part = dot_nt(ones, dpre)
    row_tiles = in_dim // 8
    for kind in range(2):
        for rt in range(row_tiles):
            src = (rt * 8 // fr) * 2 * fr + kind * fr + (rt * 8) % fr
            for c in range(2):
                n = rt * 2 + c
                part[kind, n // tpq, (n % tpq) * 8 : (n % tpq + 1) * 8, :] = grads[
                    src : src + 8, c * 128 : (c + 1) * 128
                ]
        for n in range(xz):
            part[kind, n, 8 * tpq : 8 * tpq + 1, :] = bias_part[
                0:1, kind * 128 : (kind + 1) * 128
            ]
    swap = remote(part.at[1 - core], part_recv, core_sem.at[0], core_sem.at[1], sibling)
    swap.start()
    sends.append(swap)

    act_in = []
    for i, p in enumerate(y_peers):
        act_in.append(
            remote(
                act.at[p],
                activated.at[:, pl.ds(pl.multiple_of(fy * vc, vc), vc)],
                act_sem.at[0, i],
                act_sem.at[1, i],
                (dom, p),
            )
        )
        act_in[-1].start()
    sends += act_in
    own_act = pltpu.make_async_copy(
        act.at[fy], activated.at[:, pl.ds(pl.multiple_of(fy * vc, vc), vc)], own_sem.at[2]
    )
    own_act.start()

    swap.wait_recv()
    rs_src[...] = part[core] + part_recv[...]
    rs_in = []
    for i, p in enumerate(xz_peers):
        rs_in.append(
            remote(
                rs_src.at[p],
                rs_recv.at[q],
                rs_sem.at[0, i],
                rs_sem.at[1, i],
                (p * CORES + core, fy),
            )
        )
        rs_in[-1].start()
    sends += rs_in
    rs_recv[q] = rs_src[q]

    for copy in back_in:
        copy.wait_recv()
    for b in range(nb):
        btab[b] = bkr[b // vb, fr : 2 * fr, (b % vb) * BLOCK : (b % vb + 1) * BLOCK]

    def far_body(t, sums):
        p = dot_nn(btab[tile_rows[t]], tiles[t])
        prod[t] = p
        s = slots[t] - nb
        return tuple(jnp.where(s == b, v + p, v) for b, v in enumerate(sums))

    sums = lax.fori_loop(0, tile_count, far_body, (zero,) * 16, unroll=8)
    for n in range(16):
        rb_send[n // 4, n % 4] = sums[n]
    ret = []
    for pos in range(4):
        to = lax.rem(dom + dom_size - offsets[pos], dom_size)
        ret.append(
            remote(
                rb_send.at[pos],
                rb_recv.at[pos],
                ret_sem.at[0, pos],
                ret_sem.at[1, pos],
                (to, fy),
            )
        )
        ret[-1].start()
    sends += ret

    for copy in rs_in:
        copy.wait_recv()
    total = rs_recv[0]
    for n in range(1, xz):
        total = total + rs_recv[n]
    y_src[...] = total
    y_recv[fy] = total
    y_in = []
    for i, p in enumerate(y_peers):
        y_in.append(
            remote(y_src, y_recv.at[fy], yr_sem.at[0, i], yr_sem.at[1, i], (dom, p))
        )
        y_in[-1].start()
    sends += y_in

    def near_body(t, sums):
        p = prod[t]
        s = slots[t]
        return tuple(jnp.where(s == b, v + p, v) for b, v in enumerate(sums))

    start = tuple(
        bkr[b // vb, 0:fr, (b % vb) * BLOCK : (b % vb + 1) * BLOCK].astype(F32)
        for b in range(nb)
    )
    sums = lax.fori_loop(0, tile_count, near_body, start, unroll=8)

    for copy in ret:
        copy.wait_recv()
    for pos in range(4):
        for c in range(4):
            term = rb_recv[pos, c]
            sums = tuple(
                jnp.where(owners[pos][c] == b, v + term, v) for b, v in enumerate(sums)
            )
    for b in range(nb):
        grad_features[:, b * BLOCK : (b + 1) * BLOCK] = sums[b].astype(BF16)

    for copy in y_in:
        copy.wait_recv()
    total = y_recv[0]
    for n in range(1, y_size):
        total = total + y_recv[n]
    total = total * norm_scale
    g_full[core, q] = total[: 8 * tpq]
    b_full[core] = total[8 * tpq : 8 * tpq + 1]
    bias_swap = remote(
        b_full.at[core], b_full.at[core], core_sem.at[2], core_sem.at[3], sibling
    )
    bias_swap.start()
    sends.append(bias_swap)
    ag_in = []
    for i, p in enumerate(xz_peers):
        ag_in.append(
            remote(
                g_full.at[core, q],
                g_full.at[core, q],
                ag_sem.at[0, i],
                ag_sem.at[1, i],
                (p * CORES + core, fy),
            )
        )
        ag_in[-1].start()
    sends += ag_in
    for copy in ag_in:
        copy.wait_recv()
    full_swap = remote(
        g_full.at[core], g_full.at[core], core_sem.at[4], core_sem.at[5], sibling
    )
    full_swap.start()
    sends.append(full_swap)
    own_act.wait()
    for copy in act_in:
        copy.wait_recv()
    bias_swap.wait_recv()
    for kind in range(2):
        grad_bias[:, kind * 128 : (kind + 1) * 128] = b_full[kind]
    full_swap.wait_recv()
    for kind, out in ((0, grad_self), (1, grad_neigh)):
        for rt in range(row_tiles):
            for c in range(2):
                n = rt * 2 + c
                out[rt * 8 : (rt + 1) * 8, c * 128 : (c + 1) * 128] = g_full[
                    kind, n // tpq, (n % tpq) * 8 : (n % tpq + 1) * 8, :
                ]
    for copy in sends:
        copy.wait_send()


def local(
    features,
    self_weight,
    neigh_weight,
    bias_vector,
    tile_values,
    tile_rows,
    tile_cols,
    send_blocks,
    cotangent,
):
    dom_size = lax.axis_size("dom")
    y_size = lax.axis_size("feat")
    xz = dom_size // CORES
    fr, vertices = features.shape
    hr = cotangent.shape[0]
    in_dim, hidden = self_weight.shape
    tile_count = tile_values.shape[0]
    nb = vertices // BLOCK
    vc = vertices // y_size
    tpq = (in_dim // 8) * (hidden // 128) // xz
    ext = 8 * tpq + 1
    dims = (
        dom_size,
        y_size,
        nb,
        tile_count,
        in_dim,
        hidden,
        1.0 / math.sqrt(vertices * dom_size),
    )
    smem = pl.BlockSpec(memory_space=pltpu.SMEM)
    hbm = pl.BlockSpec(memory_space=pl.ANY)
    vmem = pl.BlockSpec(memory_space=pltpu.VMEM)
    dma = pltpu.SemaphoreType.DMA
    outs = pl.pallas_call(
        functools.partial(kernel, dims),
        out_shape=(
            jax.ShapeDtypeStruct((hr, vertices), BF16),
            jax.ShapeDtypeStruct((fr, vertices), BF16),
            jax.ShapeDtypeStruct((in_dim, hidden), F32),
            jax.ShapeDtypeStruct((in_dim, hidden), F32),
            jax.ShapeDtypeStruct((1, hidden), F32),
        ),
        in_specs=[smem, smem, smem] + [hbm] * 6,
        out_specs=(hbm, vmem, vmem, vmem, vmem),
        scratch_shapes=[
            pltpu.SMEM((tile_count,), jnp.int32),
            pltpu.VMEM((fr, vertices), BF16),
            pltpu.VMEM((tile_count, BLOCK, BLOCK), BF16),
            pltpu.VMEM((in_dim, hidden), BF16),
            pltpu.VMEM((in_dim, hidden), BF16),
            pltpu.VMEM((y_size, 2, fr, hidden), BF16),
            pltpu.VMEM((hidden, 2 * in_dim), BF16),
            pltpu.VMEM((1, hidden), F32),
            pltpu.VMEM((hidden, 128), F32),
            pltpu.VMEM((y_size, 2, fr, vc), BF16),
            pltpu.VMEM((y_size, hr, vc), BF16),
            pltpu.VMEM((nb, fr, BLOCK), BF16),
            pltpu.VMEM((nb + 16, fr, BLOCK), BF16),
            pltpu.VMEM((4, 4, fr, BLOCK), BF16),
            pltpu.VMEM((y_size, fr, vc), BF16),
            pltpu.VMEM((y_size, hr, vc), BF16),
            pltpu.VMEM((y_size, 2 * fr, vc), BF16),
            pltpu.VMEM((y_size, 2 * fr, vc), BF16),
            pltpu.VMEM((nb, fr, BLOCK), BF16),
            pltpu.VMEM((tile_count, fr, BLOCK), F32),
            pltpu.VMEM((4, 4, fr, BLOCK), F32),
            pltpu.VMEM((4, 4, fr, BLOCK), F32),
            pltpu.VMEM((2, xz, ext, 128), F32),
            pltpu.VMEM((xz, ext, 128), F32),
            pltpu.VMEM((xz, ext, 128), F32),
            pltpu.VMEM((xz, ext, 128), F32),
            pltpu.VMEM((ext, 128), F32),
            pltpu.VMEM((y_size, ext, 128), F32),
            pltpu.VMEM((2, xz, 8 * tpq, 128), F32),
            pltpu.VMEM((2, 1, 128), F32),
            dma((5,)),
            dma((3,)),
            dma((2, 4)),
            dma((2, y_size - 1)),
            dma((2, y_size - 1)),
            dma((2, y_size - 1)),
            dma((2, y_size - 1)),
            dma((2, y_size - 1)),
            dma((2, 4)),
            dma((6,)),
            dma((2, xz - 1)),
            dma((2, y_size - 1)),
            dma((2, xz - 1)),
        ],
        compiler_params=pltpu.CompilerParams(
            collective_id=0, has_side_effects=True, vmem_limit_bytes=32 * 1024 * 1024
        ),
        name="graph_layer",
    )(
        tile_rows,
        tile_cols,
        send_blocks,
        features,
        self_weight,
        neigh_weight,
        bias_vector.reshape(1, hidden),
        tile_values,
        cotangent,
    )
    activated, grad_features, grad_self, grad_neigh, grad_bias = outs
    return (activated, grad_features, grad_self, grad_neigh, grad_bias.reshape(hidden))


def solution(mesh):
    in_specs = (
        P("feat", "dom"),
        P(),
        P(),
        P(),
        P("dom", None, None),
        P("dom"),
        P("dom"),
        P("dom", None, None),
        P("feat", "dom"),
    )
    out_specs = (P("feat", "dom"), P("feat", "dom"), P(), P(), P())
    return jax.shard_map(local, mesh=mesh, in_specs=in_specs, out_specs=out_specs, check_vma=False)
```

time: 610 us -> 66 us (0.11)
  waiting for transfers between devices: 366 us -> 0 us
  blocking collectives: 135 us -> 0 us
  Pallas kernels: 0 us -> 54 us
  other arithmetic: 39.4 us -> 0 us
  starting transfers between devices: 31 us -> 0 us
  between operations: 14 us -> 0.65 us
  matrix products: 11.6 us -> 0 us
    psum x1 -> x0, waiting for transfers between devices: 263 us -> none  [local(): lax.psum((part_self, part_neigh, part_bias), ('dom', 'feat'))]
    psum x1 -> x0, blocking collectives: 135 us -> none  [local(): lax.psum((part_self, part_neigh, part_bias), ('dom', 'feat'))]
    pallas_call x0 -> x1, Pallas kernels: none -> 54 us  [local(): pl.pallas_call(functools.partial(kernel, dims), out_shape=(jax.ShapeDtype...]
    all_gather x1 -> x0, waiting for transfers between devices: 40.1 us -> none  [local(): full_dpre = lax.all_gather(dpre, 'feat', axis=0, tiled=True)]
    reduce_scatter x1 -> x0, waiting for transfers between devices: 37 us -> none  [local(): lax.psum_scatter(term + jnp.einsum('fh,fv->hv', neigh_rows, agg, preferre...]
    scatter-add x3 -> x0, other arithmetic: 31.3 us -> none  [the longest x1 20.8 us: local(): from_peers = jnp.zeros((block_count, feat_rows, block_size), jnp.float32)...]
    all_to_all x2 -> x0, starting transfers between devices: 30.9 us -> none  [the longest x1 16.1 us: local(): lax.all_to_all(returned.reshape(dom_size, slot_count, feat_rows, block_si...]
    all_to_all x2 -> x0, waiting for transfers between devices: 25.4 us -> none  [the longest x1 25.4 us: local(): lax.all_to_all(outgoing, 'dom', split_axis=0, concat_axis=0, tiled=True)]
  transfers between devices with their start and end apart: 5 -> 0, of which waited for: 4 -> 0; matrix products, arithmetic and copies ran while one was open for 1% -> 0% of each run, Pallas kernels for 0% -> 0%
where the time goes in v1:
time: 66 us; the launch traced here: 65.6 us
  Pallas kernels  54 us (82%)
  local copies, waits for them, and re-layouts  10.9 us (17%)
    pallas_call x1, Pallas kernels, local(): pl.pallas_call(functools.partial(kernel, dims), out_shape=(jax.ShapeDtype...  54 us
    unnamed x22, local copies, waits for them, and re-layouts  10.9 us

profile of v1, /device:TPU:1, one launch (start us, length us, event | category | flops | bytes accessed | tf_op | source)
XLA Modules:
  0.0 65.6 jit_solution(5326171486777347421)
XLA Ops:
  0.6 0.8 %copy.14.send_blocks = s32[1,64,4]{2,1,0:T(8,128)S(1)} copy(s32[1,64,4]{1,2,0:T(4,128)} %param.16) | data formatting | bytes 2048 | tf_op args[7]
  1.4 0.0 copy-start
  1.4 1.6 %copy-done = bf16[64,128,128]{2,1,0:T(8,128)(2,1)S(1)} copy-done((bf16[64,128,128]{2,1,0:T(8,128)(2,1)S(1)}, bf16[64,128,128]{2,1,0:T(8,128)(2,1)}, u32[]{:S(2)}) %copy-start) | copy-done | bytes 2097176
  3.0 0.0 copy-start.1
  3.0 0.9 %copy-done.1 = bf16[32,2048]{1,0:T(8,128)(2,1)S(1)} copy-done((bf16[32,2048]{1,0:T(8,128)(2,1)S(1)}, bf16[32,2048]{1,0:T(8,128)(2,1)}, u32[]{:S(2)}) %copy-start.1) | copy-done | bytes 131096
  3.9 0.0 copy-start.2
  3.9 0.8 %copy-done.2 = bf16[16,2048]{1,0:T(8,128)(2,1)S(1)} copy-done((bf16[16,2048]{1,0:T(8,128)(2,1)S(1)}, bf16[16,2048]{1,0:T(8,128)(2,1)}, u32[]{:S(2)}) %copy-start.2) | copy-done | bytes 65560
  4.7 0.0 copy-start.3
  4.7 0.8 %copy-done.3 = bf16[128,256]{1,0:T(8,128)(2,1)S(1)} copy-done((bf16[128,256]{1,0:T(8,128)(2,1)S(1)}, bf16[128,256]{1,0:T(8,128)(2,1)}, u32[]{:S(2)}) %copy-start.3) | copy-done | bytes 65560
  5.6 0.0 copy-start.4
  5.6 0.8 %copy-done.4 = bf16[128,256]{1,0:T(8,128)(2,1)S(1)} copy-done((bf16[128,256]{1,0:T(8,128)(2,1)S(1)}, bf16[128,256]{1,0:T(8,128)(2,1)}, u32[]{:S(2)}) %copy-start.4) | copy-done | bytes 65560
  6.4 0.0 copy-start.5
  6.4 0.7 %copy-done.5 = f32[256]{0:T(256)S(1)} copy-done((f32[256]{0:T(256)S(1)}, f32[256]{0:T(256)}, u32[]{:S(2)}) %copy-start.5) | copy-done | bytes 1048
  7.1 0.0 copy-start.6
  7.1 0.7 copy-done.6
  7.8 0.0 copy-start.7
  7.8 0.7 copy-done.7
  8.4 54.0 %graph_layer.1 = (bf16[32,2048]{1,0:T(8,128)(2,1)S(1)}, bf16[16,2048]{1,0:T(8,128)(2,1)S(1)}, f32[128,256]{1,0:T(8,128)S(1)}, f32[128,256]{1,0:T(8,128)S(1)}, f32[1,256]{1,0:T(1,128)S(1)}) custom-call(s32[64]{0:T(128)S(1)} %copy-done.6, s32[64]{0:T(128)S(1)} %copy-done.7, s32[1,64,4]{2,1,0:T(8,128)S(1)} %copy.14.send_blocks, bf16[16,2048]{1,0:T(8,128)(2,1)S(1)} %copy-done.2, ...), custom_call_target="tpu_custom_call" | custom-call | tf_op jit(solution)/shard_map/graph_layer/pallas_call | solution.py:493
  62.4 0.7 %copy.20 = bf16[32,2048]{1,0:T(8,128)(2,1)} copy(bf16[32,2048]{1,0:T(8,128)(2,1)S(1)} %get-tuple-element.20) | data formatting | bytes 262144
  63.1 0.6 copy.21
  63.7 0.7 copy.22
  64.4 0.7 copy.23
  65.0 0.6 copy.24
Async XLA Ops:
  1.4 1.6 %copy-start = (bf16[64,128,128]{2,1,0:T(8,128)(2,1)S(1)}, bf16[64,128,128]{2,1,0:T(8,128)(2,1)}, u32[]{:S(2)}) copy-start(bf16[64,128,128]{2,1,0:T(8,128)(2,1)} %tile_values.1) | copy-start | bytes 6291460
  3.0 0.9 %copy-start.1 = (bf16[32,2048]{1,0:T(8,128)(2,1)S(1)}, bf16[32,2048]{1,0:T(8,128)(2,1)}, u32[]{:S(2)}) copy-start(bf16[32,2048]{1,0:T(8,128)(2,1)} %cotangent.1) | copy-start | bytes 393220
  3.9 0.8 %copy-start.2 = (bf16[16,2048]{1,0:T(8,128)(2,1)S(1)}, bf16[16,2048]{1,0:T(8,128)(2,1)}, u32[]{:S(2)}) copy-start(bf16[16,2048]{1,0:T(8,128)(2,1)} %features.1) | copy-start | bytes 196612
  4.7 0.8 %copy-start.3 = (bf16[128,256]{1,0:T(8,128)(2,1)S(1)}, bf16[128,256]{1,0:T(8,128)(2,1)}, u32[]{:S(2)}) copy-start(bf16[128,256]{1,0:T(8,128)(2,1)} %self_weight.1) | copy-start | bytes 196612
  5.6 0.8 %copy-start.4 = (bf16[128,256]{1,0:T(8,128)(2,1)S(1)}, bf16[128,256]{1,0:T(8,128)(2,1)}, u32[]{:S(2)}) copy-start(bf16[128,256]{1,0:T(8,128)(2,1)} %neigh_weight.1) | copy-start | bytes 196612
  6.4 0.7 %copy-start.5 = (f32[256]{0:T(256)S(1)}, f32[256]{0:T(256)}, u32[]{:S(2)}) copy-start(f32[256]{0:T(256)} %param.12) | copy-start | bytes 3076
  7.1 0.7 copy-start.6
  7.8 0.7 copy-start.7

commit v2 on v1

--- a/solution.py
+++ b/solution.py
@@ -37,9 +37,9 @@
 
 def kernel(
     dims,
-    tile_rows,
-    tile_cols,
-    send_blocks,
+    rows_in,
+    cols_in,
+    blocks_in,
     features,
     self_weight,
     neigh_weight,
@@ -51,7 +51,14 @@
     grad_self,
     grad_neigh,
     grad_bias,
+    tile_rows,
+    tile_cols,
+    send_blocks,
     slots,
+    gf,
+    gs,
+    gn,
+    gb,
     fv,
     tiles,
     w_self,
@@ -94,6 +101,7 @@
     rs_sem,
     yr_sem,
     ag_sem,
+    swap_sem,
 ):
     dom_size, y_size, nb, tile_count, in_dim, hidden, norm_scale = dims
     z_size = dom_size // (X_SIZE * CORES)
@@ -123,7 +131,10 @@
                 xz_peers.append(pz * X_SIZE + px)
 
     loads = [
+        pltpu.make_async_copy(blocks_in, send_blocks, local_sem.at[5]),
         pltpu.make_async_copy(features, fv, local_sem.at[0]),
+        pltpu.make_async_copy(cols_in, tile_cols, local_sem.at[6]),
+        pltpu.make_async_copy(rows_in, tile_rows, local_sem.at[7]),
         pltpu.make_async_copy(self_weight, w_self, local_sem.at[1]),
         pltpu.make_async_copy(neigh_weight, w_neigh, local_sem.at[2]),
         pltpu.make_async_copy(bias, bias_row, local_sem.at[3]),
@@ -150,6 +161,70 @@
         )
         greeted += 1
 
+    loads[0].wait()
+    owners = []
+    for pos in range(4):
+        to = lax.rem(dom + offsets[pos], dom_size)
+        owners.append([send_blocks[0, c, to] for c in range(4)])
+    loads[1].wait()
+    for b in range(nb):
+        own_tab[b] = fv[:, b * BLOCK : (b + 1) * BLOCK]
+    for pos in range(4):
+        for c in range(4):
+            stage[pos, c] = own_tab[jnp.maximum(owners[pos][c], 0)]
+
+    pl.semaphore_wait(barrier, greeted)
+
+    sends = []
+    halo = []
+    for pos in range(4):
+        to = lax.rem(dom + offsets[pos], dom_size)
+        halo.append(
+            remote(
+                stage.at[pos],
+                tab.at[pl.ds(nb + 4 * pos, 4)],
+                halo_sem.at[0, pos],
+                halo_sem.at[1, pos],
+                (to, fy),
+            )
+        )
+        halo[-1].start()
+    sends += halo
+    feat_in = []
+    for i, p in enumerate(y_peers):
+        feat_in.append(
+            remote(
+                fv.at[:, pl.ds(pl.multiple_of(p * vc, vc), vc)],
+                xg.at[fy, 0],
+                feat_sem.at[0, i],
+                feat_sem.at[1, i],
+                (dom, p),
+            )
+        )
+        feat_in[-1].start()
+    sends += feat_in
+    cot_in = []
+    for i, p in enumerate(y_peers):
+        cot_in.append(
+            remote(
+                cotangent.at[:, pl.ds(pl.multiple_of(p * vc, vc), vc)],
+                ct.at[fy],
+                cot_sem.at[0, i],
+                cot_sem.at[1, i],
+                (dom, p),
+            )
+        )
+        cot_in[-1].start()
+    sends += cot_in
+    own_feat = pltpu.make_async_copy(
+        fv.at[:, pl.ds(pl.multiple_of(fy * vc, vc), vc)], xg.at[fy, 0], own_sem.at[0]
+    )
+    own_feat.start()
+    own_cot = pltpu.make_async_copy(
+        cotangent.at[:, pl.ds(pl.multiple_of(fy * vc, vc), vc)], ct.at[fy], own_sem.at[1]
+    )
+    own_cot.start()
+
     def slot_body(t, carry):
         col = tile_cols[t]
         far = jnp.maximum(col - nb, 0)
@@ -162,73 +237,14 @@
         slots[t] = jnp.where(col < nb, col, nb + place * 4 + lax.rem(far, 4))
         return carry
 
-    lax.fori_loop(0, tile_count, slot_body, 0)
-
-    owners = []
-    for pos in range(4):
-        to = lax.rem(dom + offsets[pos], dom_size)
-        owners.append([send_blocks[0, to, c] for c in range(4)])
-    loads[0].wait()
+    loads[2].wait()
+    loads[3].wait()
+    lax.fori_loop(0, tile_count, slot_body, 0, unroll=4)
+
     for b in range(nb):
-        own_tab[b] = fv[:, b * BLOCK : (b + 1) * BLOCK]
         tab[b] = fv[:, b * BLOCK : (b + 1) * BLOCK]
-    for pos in range(4):
-        for c in range(4):
-            stage[pos, c] = own_tab[jnp.maximum(owners[pos][c], 0)]
-
-    pl.semaphore_wait(barrier, greeted)
-
-    sends = []
-    halo = []
-    for pos in range(4):
-        to = lax.rem(dom + offsets[pos], dom_size)
-        halo.append(
-            remote(
-                stage.at[pos],
-                tab.at[pl.ds(nb + 4 * pos, 4)],
-                halo_sem.at[0, pos],
-                halo_sem.at[1, pos],
-                (to, fy),
-            )
-        )
-        halo[-1].start()
-    sends += halo
-    feat_in = []
-    for i, p in enumerate(y_peers):
-        feat_in.append(
-            remote(
-                fv.at[:, pl.ds(pl.multiple_of(p * vc, vc), vc)],
-                xg.at[fy, 0],
-                feat_sem.at[0, i],
-                feat_sem.at[1, i],
-                (dom, p),
-            )
-        )
-        feat_in[-1].start()
-    sends += feat_in
-    cot_in = []
-    for i, p in enumerate(y_peers):
-        cot_in.append(
-            remote(
-                cotangent.at[:, pl.ds(pl.multiple_of(p * vc, vc), vc)],
-                ct.at[fy],
-                cot_sem.at[0, i],
-                cot_sem.at[1, i],
-                (dom, p),
-            )
-        )
-        cot_in[-1].start()
-    sends += cot_in
-    own_feat = pltpu.make_async_copy(
-        fv.at[:, pl.ds(pl.multiple_of(fy * vc, vc), vc)], xg.at[fy, 0], own_sem.at[0]
-    )
-    own_feat.start()
-    own_cot = pltpu.make_async_copy(
-        cotangent.at[:, pl.ds(pl.multiple_of(fy * vc, vc), vc)], ct.at[fy], own_sem.at[1]
-    )
-    own_cot.start()
-
-    for copy in loads[1:4]:
+
+    for copy in loads[4:7]:
         copy.wait()
     for y in range(y_size):
         w_cat[y, 0] = w_self[y * fr : (y + 1) * fr, :]
@@ -236,7 +252,7 @@
     weights = w_cat[...].reshape(2 * in_dim, hidden)
     w_t[...] = weights.astype(F32).T.astype(BF16)
     bias_mat[...] = jnp.broadcast_to(bias_row[...], (128, hidden)).T
-    loads[4].wait()
+    loads[7].wait()
 
     for copy in halo:
         copy.wait_recv()
@@ -271,18 +287,6 @@
     sigma = jax.nn.sigmoid(pre)
     cot = ct[...].reshape(hidden, vc).astype(F32)
     dpre = (cot * sigma * (1.0 + pre * (1.0 - sigma))).astype(BF16)
-    act[...] = (pre * sigma).astype(BF16).reshape(y_size, hr, vc)
-    bk[...] = dot_nn(weights, dpre).astype(BF16).reshape(y_size, 2 * fr, vc)
-
-    back_in = []
-    for i, p in enumerate(y_peers):
-        back_in.append(
-            remote(bk.at[p], bkr.at[fy], back_sem.at[0, i], back_sem.at[1, i], (dom, p))
-        )
-        back_in[-1].start()
-    sends += back_in
-    bkr[fy] = bk[fy]
-
     grads = dot_nt(both, dpre)
     ones = jnp.ones((16, vc), BF16)
     bias_part = dot_nt(ones, dpre)
@@ -303,6 +307,35 @@
     swap.start()
     sends.append(swap)
 
+    act[...] = (pre * sigma).astype(BF16).reshape(y_size, hr, vc)
+    bk[...] = dot_nn(weights, dpre).astype(BF16).reshape(y_size, 2 * fr, vc)
+
+    back_in = []
+    for i, p in enumerate(y_peers):
+        back_in.append(
+            remote(bk.at[p], bkr.at[fy], back_sem.at[0, i], back_sem.at[1, i], (dom, p))
+        )
+        back_in[-1].start()
+    sends += back_in
+    bkr[fy] = bk[fy]
+
+    swap.wait_recv()
+    rs_src[...] = part[core] + part_recv[...]
+    rs_in = []
+    for i, p in enumerate(xz_peers):
+        rs_in.append(
+            remote(
+                rs_src.at[p],
+                rs_recv.at[q],
+                rs_sem.at[0, i],
+                rs_sem.at[1, i],
+                (p * CORES + core, fy),
+            )
+        )
+        rs_in[-1].start()
+    sends += rs_in
+    rs_recv[q] = rs_src[q]
+
     act_in = []
     for i, p in enumerate(y_peers):
         act_in.append(
@@ -320,23 +353,6 @@
         act.at[fy], activated.at[:, pl.ds(pl.multiple_of(fy * vc, vc), vc)], own_sem.at[2]
     )
     own_act.start()
-
-    swap.wait_recv()
-    rs_src[...] = part[core] + part_recv[...]
-    rs_in = []
-    for i, p in enumerate(xz_peers):
-        rs_in.append(
-            remote(
-                rs_src.at[p],
-                rs_recv.at[q],
-                rs_sem.at[0, i],
-                rs_sem.at[1, i],
-                (p * CORES + core, fy),
-            )
-        )
-        rs_in[-1].start()
-    sends += rs_in
-    rs_recv[q] = rs_src[q]
 
     for copy in back_in:
         copy.wait_recv()
@@ -402,7 +418,9 @@
                 jnp.where(owners[pos][c] == b, v + term, v) for b, v in enumerate(sums)
             )
     for b in range(nb):
-        grad_features[:, b * BLOCK : (b + 1) * BLOCK] = sums[b].astype(BF16)
+        gf[:, b * BLOCK : (b + 1) * BLOCK] = sums[b].astype(BF16)
+    stores = [pltpu.make_async_copy(gf, grad_features, local_sem.at[0])]
+    stores[0].start()
 
     for copy in y_in:
         copy.wait_recv()
@@ -430,29 +448,57 @@
         )
         ag_in[-1].start()
     sends += ag_in
-    for copy in ag_in:
-        copy.wait_recv()
-    full_swap = remote(
-        g_full.at[core], g_full.at[core], core_sem.at[4], core_sem.at[5], sibling
-    )
-    full_swap.start()
-    sends.append(full_swap)
-    own_act.wait()
-    for copy in act_in:
-        copy.wait_recv()
+    swaps = []
+    for dz in range(z_size):
+        for copy in ag_in[max(dz * X_SIZE - 1, 0) : (dz + 1) * X_SIZE - 1]:
+            copy.wait_recv()
+        plane = pl.ds(lax.rem(my_z + z_size - dz, z_size) * X_SIZE, X_SIZE)
+        swaps.append(
+            remote(
+                g_full.at[core, plane],
+                g_full.at[core, plane],
+                swap_sem.at[0, dz],
+                swap_sem.at[1, dz],
+                sibling,
+            )
+        )
+        swaps[-1].start()
+    sends += swaps
     bias_swap.wait_recv()
     for kind in range(2):
-        grad_bias[:, kind * 128 : (kind + 1) * 128] = b_full[kind]
-    full_swap.wait_recv()
-    for kind, out in ((0, grad_self), (1, grad_neigh)):
+        gb[:, kind * 128 : (kind + 1) * 128] = b_full[kind]
+    for copy in swaps:
+        copy.wait_recv()
+    for kind, out in ((0, gs), (1, gn)):
         for rt in range(row_tiles):
             for c in range(2):
                 n = rt * 2 + c
                 out[rt * 8 : (rt + 1) * 8, c * 128 : (c + 1) * 128] = g_full[
                     kind, n // tpq, (n % tpq) * 8 : (n % tpq + 1) * 8, :
                 ]
+    stores += [
+        pltpu.make_async_copy(gs, grad_self, local_sem.at[1]),
+        pltpu.make_async_copy(gn, grad_neigh, local_sem.at[2]),
+        pltpu.make_async_copy(gb, grad_bias, local_sem.at[3]),
+    ]
+    for copy in stores[1:]:
+        copy.start()
+    own_act.wait()
+    for copy in act_in:
+        copy.wait_recv()
+    for copy in stores:
+        copy.wait()
     for copy in sends:
         copy.wait_send()
+
+
+def place(*refs):
+    sems = refs[10]
+    copies = [pltpu.make_async_copy(refs[i], refs[5 + i], sems.at[i]) for i in range(5)]
+    for copy in copies:
+        copy.start()
+    for copy in copies:
+        copy.wait()
 
 
 def local(
@@ -486,9 +532,7 @@
         hidden,
         1.0 / math.sqrt(vertices * dom_size),
     )
-    smem = pl.BlockSpec(memory_space=pltpu.SMEM)
     hbm = pl.BlockSpec(memory_space=pl.ANY)
-    vmem = pl.BlockSpec(memory_space=pltpu.VMEM)
     dma = pltpu.SemaphoreType.DMA
     outs = pl.pallas_call(
         functools.partial(kernel, dims),
@@ -499,10 +543,17 @@
             jax.ShapeDtypeStruct((in_dim, hidden), F32),
             jax.ShapeDtypeStruct((1, hidden), F32),
         ),
-        in_specs=[smem, smem, smem] + [hbm] * 6,
-        out_specs=(hbm, vmem, vmem, vmem, vmem),
+        in_specs=[hbm] * 9,
+        out_specs=(hbm,) * 5,
         scratch_shapes=[
             pltpu.SMEM((tile_count,), jnp.int32),
+            pltpu.SMEM((tile_count,), jnp.int32),
+            pltpu.SMEM((1, 4, dom_size), jnp.int32),
+            pltpu.SMEM((tile_count,), jnp.int32),
+            pltpu.VMEM((fr, vertices), BF16),
+            pltpu.VMEM((in_dim, hidden), F32),
+            pltpu.VMEM((in_dim, hidden), F32),
+            pltpu.VMEM((1, hidden), F32),
             pltpu.VMEM((fr, vertices), BF16),
             pltpu.VMEM((tile_count, BLOCK, BLOCK), BF16),
             pltpu.VMEM((in_dim, hidden), BF16),
@@ -532,7 +583,7 @@
             pltpu.VMEM((y_size, ext, 128), F32),
             pltpu.VMEM((2, xz, 8 * tpq, 128), F32),
             pltpu.VMEM((2, 1, 128), F32),
-            dma((5,)),
+            dma((8,)),
             dma((3,)),
             dma((2, 4)),
             dma((2, y_size - 1)),
@@ -545,15 +596,16 @@
             dma((2, xz - 1)),
             dma((2, y_size - 1)),
             dma((2, xz - 1)),
+            dma((2, xz // X_SIZE)),
         ],
         compiler_params=pltpu.CompilerParams(
-            collective_id=0, has_side_effects=True, vmem_limit_bytes=32 * 1024 * 1024
+            collective_id=0, has_side_effects=True, vmem_limit_bytes=56 * 1024 * 1024
         ),
         name="graph_layer",
     )(
         tile_rows,
         tile_cols,
-        send_blocks,
+        send_blocks.transpose(0, 2, 1),
         features,
         self_weight,
         neigh_weight,
@@ -561,6 +613,15 @@
         tile_values,
         cotangent,
     )
+    outs = pl.pallas_call(
+        place,
+        out_shape=tuple(jax.ShapeDtypeStruct(o.shape, o.dtype) for o in outs),
+        in_specs=[hbm] * 5,
+        out_specs=(hbm,) * 5,
+        scratch_shapes=[dma((5,))],
+        compiler_params=pltpu.CompilerParams(vmem_limit_bytes=56 * 1024 * 1024),
+        name="place_outputs",
+    )(*outs)
     activated, grad_features, grad_self, grad_neigh, grad_bias = outs
     return (activated, grad_features, grad_self, grad_neigh, grad_bias.reshape(hidden))
 

time: 66 us -> 70.1 us (1.062)
  Pallas kernels: 54 us -> 69.3 us
  local copies, waits for them, and re-layouts: 10.9 us -> 0 us
    pallas_call x0 -> x1, Pallas kernels: none -> 15.1 us  [local(): pl.pallas_call(place, out_shape=tuple((jax.ShapeDtypeStruct(o.shape, o.dt...]
    unnamed x22 -> x0, local copies, waits for them, and re-layouts: 10.9 us -> none
where the time goes in v2:
time: 70.1 us; the launch traced here: 70 us
  Pallas kernels  69.3 us (99%)
    pallas_call x1, Pallas kernels, local(): pl.pallas_call(functools.partial(kernel, dims), out_shape=(jax.ShapeDtype...  54.3 us
    pallas_call x1, Pallas kernels, local(): pl.pallas_call(place, out_shape=tuple((jax.ShapeDtypeStruct(o.shape, o.dt...  15.1 us

profile of v2, /device:TPU:1, one launch (start us, length us, event | category | flops | bytes accessed | tf_op | source)
XLA Modules:
  0.0 70.0 jit_solution(1638746907959156819)
XLA Ops:
  0.6 54.3 %graph_layer.1 = (bf16[32,2048]{1,0:T(8,128)(2,1)}, bf16[16,2048]{1,0:T(8,128)(2,1)}, f32[128,256]{1,0:T(8,128)}, f32[128,256]{1,0:T(8,128)}, f32[1,256]{1,0:T(1,128)}) custom-call(s32[64]{0:T(128)} %rows_in.1, s32[64]{0:T(128)} %cols_in.1, s32[1,4,64]{2,1,0:T(4,128)} %bitcast.3, bf16[16,2048]{1,0:T(8,128)(2,1)} %features.1, bf16[128,256]{1,0:T(8,128)(2,1)} %self_weight.1, ...), custom_call_target="tpu_custom_call" | custom-call | tf_op jit(solution)/shard_map/graph_layer/pallas_call | solution.py:537
  54.9 15.1 %place_outputs.1 = (bf16[32,2048]{1,0:T(8,128)(2,1)}, bf16[16,2048]{1,0:T(8,128)(2,1)}, f32[128,256]{1,0:T(8,128)}, f32[128,256]{1,0:T(8,128)}, f32[1,256]{1,0:T(1,128)}) custom-call(bf16[32,2048]{1,0:T(8,128)(2,1)} %get-tuple-element.15.refs_0_, bf16[16,2048]{1,0:T(8,128)(2,1)} %get-tuple-element.16.refs_1_, f32[128,256]{1,0:T(8,128)} %get-tuple-element.17.refs_2_, ...), custom_call_target="tpu_custom_call" | custom-call | tf_op jit(solution)/shard_map/place_outputs/pallas_call | solution.py:616

commit v3 on v2

v3 whole, which is shorter than its diff:
```python
import functools
import math

import jax
import jax.numpy as jnp
from jax import lax
from jax.experimental import pallas as pl
from jax.experimental.pallas import tpu as pltpu
from jax.sharding import PartitionSpec as P

X_SIZE = 4
CORES = 2
BLOCK = 128
MESH = pl.DeviceIdType.MESH
F32 = jnp.float32
BF16 = jnp.bfloat16


def remote(src, dst, send_sem, recv_sem, device):
    return pltpu.make_async_remote_copy(
        src_ref=src,
        dst_ref=dst,
        send_sem=send_sem,
        recv_sem=recv_sem,
        device_id=device,
        device_id_type=MESH,
    )


def dot_nt(a, b):
    return lax.dot_general(a, b, (((1,), (1,)), ((), ())), preferred_element_type=F32)


def dot_nn(a, b):
    return lax.dot_general(a, b, (((1,), (0,)), ((), ())), preferred_element_type=F32)


def drain(ref, sem):
    pltpu.make_async_copy(ref, ref, sem).wait()


def one_hot(ids, nb, fr, base, out):
    rows = nb * fr
    per = 128 // fr
    lane = lax.broadcasted_iota(jnp.int32, (1, 128), 1)
    row = lax.broadcasted_iota(jnp.int32, (rows, 128), 0)
    for group in range(out.shape[1] // 128):
        key = jnp.zeros((1, 128), jnp.int32)
        for u in range(per):
            key = jnp.where(lane // fr == u, (ids[group * per + u] - base) * fr, key)
        key = key + lane % fr
        out[:, group * 128 : (group + 1) * 128] = jnp.where(row == key, 1.0, 0.0).astype(BF16)


def split(value):
    high = value.astype(BF16)
    return high, (value - high.astype(F32)).astype(BF16)


def kernel(
    dims,
    rows_in,
    cols_in,
    blocks_in,
    features,
    self_weight,
    neigh_weight,
    bias,
    tile_values,
    cotangent,
    activated,
    grad_features,
    grad_self,
    grad_neigh,
    grad_bias,
    tile_rows,
    tile_cols,
    send_blocks,
    slots,
    gf,
    gs,
    gn,
    gb,
    fv,
    tiles,
    w_self,
    w_neigh,
    w_cat,
    w_t,
    bias_row,
    bias_mat,
    xg,
    ct,
    own_tab,
    tab,
    stage,
    agg,
    act,
    bk,
    bkr,
    btab,
    prod,
    by_row,
    by_far,
    by_near,
    rb_send,
    rb_recv,
    part_own,
    part_send,
    part_recv,
    rs_src,
    rs_recv,
    y_src,
    y_recv,
    g_full,
    b_full,
    local_sem,
    send_sem,
    recv_sem,
    plane_sem,
):
    dom_size, y_size, nb, tile_count, in_dim, hidden, norm_scale = dims
    z_size = dom_size // (X_SIZE * CORES)
    xz = X_SIZE * z_size
    fr = in_dim // y_size
    hr = hidden // y_size
    vb = nb // y_size
    vc = vb * BLOCK
    tpq = (in_dim // 8) * (hidden // 128) // xz
    row_tiles = in_dim // 8
    others = y_size - 1

    dom = lax.axis_index("dom")
    fy = lax.axis_index("feat")
    core = lax.rem(dom, CORES)
    q = dom // CORES
    my_z = q // X_SIZE
    my_x = lax.rem(q, X_SIZE)

    offsets = (1, 2, dom_size - 1, dom_size // 2)
    y_peers = [lax.rem(fy + i, y_size) for i in range(1, y_size)]
    sibling = (q * CORES + 1 - core, fy)
    xz_peers = []
    for dz in range(z_size):
        for dx in range(X_SIZE):
            if dz or dx:
                pz = lax.rem(my_z + dz, z_size)
                px = lax.rem(my_x + dx, X_SIZE)
                xz_peers.append((dz, pz * X_SIZE + px))

    def columns(ref, y):
        return ref.at[:, pl.ds(pl.multiple_of(y * vc, vc), vc)]

    loads = [
        pltpu.make_async_copy(src, dst, local_sem.at[i])
        for i, (src, dst) in enumerate(
            (
                (blocks_in, send_blocks),
                (features, fv),
                (cols_in, tile_cols),
                (rows_in, tile_rows),
                (self_weight, w_self),
                (neigh_weight, w_neigh),
                (bias, bias_row),
                (tile_values, tiles),
            )
        )
    ]
    for copy in loads:
        copy.start()

    barrier = pltpu.get_barrier_semaphore()
    greet = [(dom, p) for p in y_peers]
    for off in (1, 2, dom_size - 1, dom_size - 2, dom_size // 2):
        greet.append((lax.rem(dom + off, dom_size), fy))
    greet.append(sibling)
    greet += [(p * CORES + core, fy) for _, p in xz_peers]
    for device in greet:
        pl.semaphore_signal(barrier, inc=1, device_id=device, device_id_type=MESH)

    loads[0].wait()
    owners = []
    for pos in range(4):
        to = lax.rem(dom + offsets[pos], dom_size)
        owners.append([send_blocks[0, c, to] for c in range(4)])
    loads[1].wait()
    for b in range(nb):
        own_tab[b] = fv[:, b * BLOCK : (b + 1) * BLOCK]
    for pos in range(4):
        for c in range(4):
            stage[pos, c] = own_tab[jnp.maximum(owners[pos][c], 0)]

    pl.semaphore_wait(barrier, len(greet))

    for pos in range(4):
        to = lax.rem(dom + offsets[pos], dom_size)
        remote(
            stage.at[pos],
            tab.at[pl.ds(nb + 4 * pos, 4)],
            send_sem.at[0],
            recv_sem.at[0],
            (to, fy),
        ).start()
    for p in y_peers:
        remote(columns(fv, p), xg.at[fy, 0], send_sem.at[1], recv_sem.at[1], (dom, p)).start()
    for p in y_peers:
        remote(columns(cotangent, p), ct.at[fy], send_sem.at[2], recv_sem.at[2], (dom, p)).start()
    own_cot = pltpu.make_async_copy(columns(cotangent, fy), ct.at[fy], local_sem.at[8])
    own_cot.start()
    xg[fy, 0] = fv[:, pl.ds(pl.multiple_of(fy * vc, vc), vc)]

    for copy in loads[2:]:
        copy.wait()

    def slot_body(t, carry):
        col = tile_cols[t]
        far = jnp.maximum(col - nb, 0)
        back = lax.rem(dom + dom_size - far // 4, dom_size)
        place = jnp.where(
            back == offsets[0],
            0,
            jnp.where(back == offsets[1], 1, jnp.where(back == offsets[2], 2, 3)),
        )
        slots[t] = jnp.where(col < nb, col, nb + place * 4 + lax.rem(far, 4))
        return carry

    lax.fori_loop(0, tile_count, slot_body, 0, unroll=4)
    for b in range(nb):
        tab[b] = fv[:, b * BLOCK : (b + 1) * BLOCK]
    one_hot(tile_rows, nb, fr, 0, by_row)

    drain(stage, recv_sem.at[0])

    def agg_body(t, carry):
        prod[t] = dot_nt(tab[slots[t]], tiles[t])
        return carry

    lax.fori_loop(0, tile_count, agg_body, 0, unroll=tile_count)
    high, low = split(prod[...].reshape(tile_count * fr, BLOCK))
    sums = (dot_nn(by_row[...], high) + dot_nn(by_row[...], low)).astype(BF16)
    for b in range(nb):
        agg[b // vb, :, (b % vb) * BLOCK : (b % vb + 1) * BLOCK] = sums[b * fr : (b + 1) * fr]
    for p in y_peers:
        remote(agg.at[p], xg.at[fy, 1], send_sem.at[3], recv_sem.at[3], (dom, p)).start()
    xg[fy, 1] = agg[fy]

    for y in range(y_size):
        w_cat[y, 0] = w_self[y * fr : (y + 1) * fr, :]
        w_cat[y, 1] = w_neigh[y * fr : (y + 1) * fr, :]
    weights = w_cat[...].reshape(2 * in_dim, hidden)
    w_t[...] = weights.astype(F32).T.astype(BF16)
    bias_mat[...] = jnp.broadcast_to(bias_row[...], (128, hidden)).T
    one_hot(slots, 16, fr, nb, by_far)
    one_hot(slots, nb, fr, 0, by_near)

    own_cot.wait()
    drain(xg.at[0:others, 0], recv_sem.at[1])
    drain(ct.at[0:others], recv_sem.at[2])
    drain(agg.at[0:others], recv_sem.at[3])

    both = xg[...].reshape(2 * in_dim, vc)
    pre = dot_nn(w_t[...], both) + jnp.concatenate([bias_mat[...]] * vb, axis=1)
    sigma = jax.nn.sigmoid(pre)
    cot = ct[...].reshape(hidden, vc).astype(F32)
    dpre = (cot * sigma * (1.0 + pre * (1.0 - sigma))).astype(BF16)

    bias_part = dot_nt(jnp.ones((16, vc), BF16), dpre)
    for kind, out in ((1 - core, part_send), (core, part_own)):
        grads = dot_nt(xg[:, kind].reshape(in_dim, vc), dpre)
        half = jnp.where(kind == 0, bias_part[0:1, 0:128], bias_part[0:1, 128:256])
        for rt in range(row_tiles):
            for c in range(2):
                n = rt * 2 + c
                out[n // tpq, (n % tpq) * 8 : (n % tpq + 1) * 8, :] = grads[
                    rt * 8 : (rt + 1) * 8, c * 128 : (c + 1) * 128
                ]
        for n in range(xz):
            out[n, 8 * tpq : 8 * tpq + 1, :] = half
        if out is part_send:
            swap = remote(part_send, part_recv, send_sem.at[4], recv_sem.at[4], sibling)
            swap.start()
    bk[...] = dot_nn(weights, dpre).astype(BF16).reshape(y_size, 2 * fr, vc)
    for p in y_peers:
        remote(bk.at[p], bkr.at[fy], send_sem.at[5], recv_sem.at[5], (dom, p)).start()
    bkr[fy] = bk[fy]
    act[...] = (pre * sigma).astype(BF16).reshape(y_size, hr, vc)

    swap.wait_recv()
    rs_src[...] = part_own[...] + part_recv[...]
    for _, p in xz_peers:
        remote(
            rs_src.at[p], rs_recv.at[q], send_sem.at[6], recv_sem.at[6], (p * CORES + core, fy)
        ).start()
    rs_recv[q] = rs_src[q]

    drain(bkr.at[0:others], recv_sem.at[5])
    for b in range(nb):
        btab[b] = bkr[b // vb, fr : 2 * fr, (b % vb) * BLOCK : (b % vb + 1) * BLOCK]

    def spread_body(t, carry):
        prod[t] = dot_nn(btab[tile_rows[t]], tiles[t])
        return carry

    lax.fori_loop(0, tile_count, spread_body, 0, unroll=tile_count)
    high, low = split(prod[...].reshape(tile_count * fr, BLOCK))
    sums = dot_nn(by_far[...], high) + dot_nn(by_far[...], low)
    for n in range(16):
        rb_send[n // 4, n % 4] = sums[n * fr : (n + 1) * fr]
    for pos in range(4):
        to = lax.rem(dom + dom_size - offsets[pos], dom_size)
        remote(
            rb_send.at[pos], rb_recv.at[pos], send_sem.at[7], recv_sem.at[7], (to, fy)
        ).start()

    drain(rs_recv.at[0 : xz - 1], recv_sem.at[6])
    total = rs_recv[0]
    for n in range(1, xz):
        total = total + rs_recv[n]
    y_src[...] = total
    y_recv[fy] = total
    for p in y_peers:
        remote(y_src, y_recv.at[fy], send_sem.at[8], recv_sem.at[8], (dom, p)).start()
    for p in y_peers:
        remote(
            act.at[p], columns(activated, fy), send_sem.at[9], recv_sem.at[9], (dom, p)
        ).start()
    own_act = pltpu.make_async_copy(act.at[fy], columns(activated, fy), local_sem.at[9])
    own_act.start()

    near = dot_nn(by_near[...], high) + dot_nn(by_near[...], low)

    drain(y_recv.at[0:others], recv_sem.at[8])
    total = y_recv[0]
    for n in range(1, y_size):
        total = total + y_recv[n]
    total = total * norm_scale
    g_full[core, q] = total[: 8 * tpq]
    b_full[core] = total[8 * tpq : 8 * tpq + 1]
    for dz, p in xz_peers:
        remote(
            g_full.at[core, q],
            g_full.at[core, q],
            send_sem.at[10],
            plane_sem.at[dz],
            (p * CORES + core, fy),
        ).start()
    bias_swap = remote(
        b_full.at[core], b_full.at[core], send_sem.at[11], recv_sem.at[9 + 1], sibling
    )
    bias_swap.start()

    drain(rb_recv, recv_sem.at[7])
    sums = [
        near[b * fr : (b + 1) * fr]
        + bkr[b // vb, 0:fr, (b % vb) * BLOCK : (b % vb + 1) * BLOCK].astype(F32)
        for b in range(nb)
    ]
    for pos in range(4):
        for c in range(4):
            term = rb_recv[pos, c]
            sums = [jnp.where(owners[pos][c] == b, v + term, v) for b, v in enumerate(sums)]
    for b in range(nb):
        gf[:, b * BLOCK : (b + 1) * BLOCK] = sums[b].astype(BF16)
    stores = [pltpu.make_async_copy(gf, grad_features, local_sem.at[0])]
    stores[0].start()

    for dz in range(z_size):
        drain(g_full.at[0, 0 : X_SIZE - (dz == 0)], plane_sem.at[dz])
        plane = pl.ds(lax.rem(my_z + z_size - dz, z_size) * X_SIZE, X_SIZE)
        remote(
            g_full.at[core, plane],
            g_full.at[core, plane],
            send_sem.at[12],
            recv_sem.at[11],
            sibling,
        ).start()
    bias_swap.wait_recv()
    for kind in range(2):
        gb[:, kind * 128 : (kind + 1) * 128] = b_full[kind]
    stores.append(pltpu.make_async_copy(gb, grad_bias, local_sem.at[1]))
    stores[1].start()
    drain(g_full.at[0], recv_sem.at[11])
    for kind, out, dst in ((0, gs, grad_self), (1, gn, grad_neigh)):
        for rt in range(row_tiles):
            for c in range(2):
                n = rt * 2 + c
                out[rt * 8 : (rt + 1) * 8, c * 128 : (c + 1) * 128] = g_full[
                    kind, n // tpq, (n % tpq) * 8 : (n % tpq + 1) * 8, :
                ]
        stores.append(pltpu.make_async_copy(out, dst, local_sem.at[2 + kind]))
        stores[-1].start()
    own_act.wait()
    drain(activated.at[:, 0 : others * vc], recv_sem.at[9])

    drain(stage, send_sem.at[0])
    drain(xg.at[0:others, 0], send_sem.at[1])
    drain(ct.at[0:others], send_sem.at[2])
    drain(agg.at[0:others], send_sem.at[3])
    swap.wait_send()
    drain(bkr.at[0:others], send_sem.at[5])
    drain(rs_recv.at[0 : xz - 1], send_sem.at[6])
    drain(rb_recv, send_sem.at[7])
    drain(y_recv.at[0:others], send_sem.at[8])
    drain(activated.at[:, 0 : others * vc], send_sem.at[9])
    drain(g_full.at[0, 0 : xz - 1], send_sem.at[10])
    bias_swap.wait_send()
    drain(g_full.at[0], send_sem.at[12])
    for copy in stores:
        copy.wait()


def place(*refs):
    count = len(refs) // 3
    sems = refs[-1]
    ins, outs, held = refs[:count], refs[count : 2 * count], refs[2 * count : 3 * count]
    first = [pltpu.make_async_copy(ins[i], held[i], sems.at[0, i]) for i in range(count)]
    second = [pltpu.make_async_copy(held[i], outs[i], sems.at[1, i]) for i in range(count)]
    for copy in first:
        copy.start()
    for a, b in zip(first, second):
        a.wait()
        b.start()
    for copy in second:
        copy.wait()


def local(
    features,
    self_weight,
    neigh_weight,
    bias_vector,
    tile_values,
    tile_rows,
    tile_cols,
    send_blocks,
    cotangent,
):
    dom_size = lax.axis_size("dom")
    y_size = lax.axis_size("feat")
    xz = dom_size // CORES
    fr, vertices = features.shape
    hr = cotangent.shape[0]
    in_dim, hidden = self_weight.shape
    tile_count = tile_values.shape[0]
    nb = vertices // BLOCK
    vc = vertices // y_size
    tpq = (in_dim // 8) * (hidden // 128) // xz
    ext = 8 * tpq + 1
    dims = (
        dom_size,
        y_size,
        nb,
        tile_count,
        in_dim,
        hidden,
        1.0 / math.sqrt(vertices * dom_size),
    )
    hbm = pl.BlockSpec(memory_space=pl.ANY)
    dma = pltpu.SemaphoreType.DMA
    outs = pl.pallas_call(
        functools.partial(kernel, dims),
        out_shape=(
            jax.ShapeDtypeStruct((hr, vertices), BF16),
            jax.ShapeDtypeStruct((fr, vertices), BF16),
            jax.ShapeDtypeStruct((in_dim, hidden), F32),
            jax.ShapeDtypeStruct((in_dim, hidden), F32),
            jax.ShapeDtypeStruct((1, hidden), F32),
        ),
        in_specs=[hbm] * 9,
        out_specs=(hbm,) * 5,
        scratch_shapes=[
            pltpu.SMEM((tile_count,), jnp.int32),
            pltpu.SMEM((tile_count,), jnp.int32),
            pltpu.SMEM((1, 4, dom_size), jnp.int32),
            pltpu.SMEM((tile_count,), jnp.int32),
            pltpu.VMEM((fr, vertices), BF16),
            pltpu.VMEM((in_dim, hidden), F32),
            pltpu.VMEM((in_dim, hidden), F32),
            pltpu.VMEM((1, hidden), F32),
            pltpu.VMEM((fr, vertices), BF16),
            pltpu.VMEM((tile_count, BLOCK, BLOCK), BF16),
            pltpu.VMEM((in_dim, hidden), BF16),
            pltpu.VMEM((in_dim, hidden), BF16),
            pltpu.VMEM((y_size, 2, fr, hidden), BF16),
            pltpu.VMEM((hidden, 2 * in_dim), BF16),
            pltpu.VMEM((1, hidden), F32),
            pltpu.VMEM((hidden, 128), F32),
            pltpu.VMEM((y_size, 2, fr, vc), BF16),
            pltpu.VMEM((y_size, hr, vc), BF16),
            pltpu.VMEM((nb, fr, BLOCK), BF16),
            pltpu.VMEM((nb + 16, fr, BLOCK), BF16),
            pltpu.VMEM((4, 4, fr, BLOCK), BF16),
            pltpu.VMEM((y_size, fr, vc), BF16),
            pltpu.VMEM((y_size, hr, vc), BF16),
            pltpu.VMEM((y_size, 2 * fr, vc), BF16),
            pltpu.VMEM((y_size, 2 * fr, vc), BF16),
            pltpu.VMEM((nb, fr, BLOCK), BF16),
            pltpu.VMEM((tile_count, fr, BLOCK), F32),
            pltpu.VMEM((nb * fr, tile_count * fr), BF16),
            pltpu.VMEM((16 * fr, tile_count * fr), BF16),
            pltpu.VMEM((nb * fr, tile_count * fr), BF16),
            pltpu.VMEM((4, 4, fr, BLOCK), F32),
            pltpu.VMEM((4, 4, fr, BLOCK), F32),
            pltpu.VMEM((xz, ext, 128), F32),
            pltpu.VMEM((xz, ext, 128), F32),
            pltpu.VMEM((xz, ext, 128), F32),
            pltpu.VMEM((xz, ext, 128), F32),
            pltpu.VMEM((xz, ext, 128), F32),
            pltpu.VMEM((ext, 128), F32),
            pltpu.VMEM((y_size, ext, 128), F32),
            pltpu.VMEM((2, xz, 8 * tpq, 128), F32),
            pltpu.VMEM((2, 1, 128), F32),
            dma((10,)),
            dma((13,)),
            dma((12,)),
            dma((xz // X_SIZE,)),
        ],
        compiler_params=pltpu.CompilerParams(
            collective_id=0, has_side_effects=True, vmem_limit_bytes=56 * 1024 * 1024
        ),
        name="graph_layer",
    )(
        tile_rows,
        tile_cols,
        send_blocks.transpose(0, 2, 1),
        features,
        self_weight,
        neigh_weight,
        bias_vector.reshape(1, hidden),
        tile_values,
        cotangent,
    )
    outs = pl.pallas_call(
        place,
        out_shape=tuple(jax.ShapeDtypeStruct(o.shape, o.dtype) for o in outs),
        in_specs=[hbm] * 5,
        out_specs=(hbm,) * 5,
        scratch_shapes=[pltpu.VMEM(o.shape, o.dtype) for o in outs] + [dma((2, 5))],
        compiler_params=pltpu.CompilerParams(vmem_limit_bytes=56 * 1024 * 1024),
        name="place_outputs",
    )(*outs)
    activated, grad_features, grad_self, grad_neigh, grad_bias = outs
    return (activated, grad_features, grad_self, grad_neigh, grad_bias.reshape(hidden))


def solution(mesh):
    in_specs = (
        P("feat", "dom"),
        P(),
        P(),
        P(),
        P("dom", None, None),
        P("dom"),
        P("dom"),
        P("dom", None, None),
        P("feat", "dom"),
    )
    out_specs = (P("feat", "dom"), P("feat", "dom"), P(), P(), P())
    return jax.shard_map(local, mesh=mesh, in_specs=in_specs, out_specs=out_specs, check_vma=False)
```

time: 70.1 us -> 52.1 us (0.74)
  Pallas kernels: 69.3 us -> 51.3 us
    pallas_call x1, Pallas kernels: 15.1 us -> 1.81 us  [local(): pl.pallas_call(place, out_shape=tuple((jax.ShapeDtypeStruct(o.shape, o.dt...]
    pallas_call x1, Pallas kernels: 54.3 us -> 49.5 us  [local(): pl.pallas_call(functools.partial(kernel, dims), out_shape=(jax.ShapeDtype...]
where the time goes in v3:
time: 52.1 us; the launch traced here: 52 us
  Pallas kernels  51.3 us (98%)
  between operations  0.64 us (1%)
    pallas_call x1, Pallas kernels, local(): pl.pallas_call(functools.partial(kernel, dims), out_shape=(jax.ShapeDtype...  49.5 us
    pallas_call x1, Pallas kernels, local(): pl.pallas_call(place, out_shape=tuple((jax.ShapeDtypeStruct(o.shape, o.dt...  1.81 us

profile of v3, /device:TPU:1, one launch (start us, length us, event | category | flops | bytes accessed | tf_op | source)
XLA Modules:
  0.0 52.0 jit_solution(3119318762289263519)
XLA Ops:
  0.6 49.5 %graph_layer.1 = (bf16[32,2048]{1,0:T(8,128)(2,1)}, bf16[16,2048]{1,0:T(8,128)(2,1)}, f32[128,256]{1,0:T(8,128)}, f32[128,256]{1,0:T(8,128)}, f32[1,256]{1,0:T(1,128)}) custom-call(s32[64]{0:T(128)} %rows_in.1, s32[64]{0:T(128)} %cols_in.1, s32[1,4,64]{2,1,0:T(4,128)} %bitcast.3, bf16[16,2048]{1,0:T(8,128)(2,1)} %features.1, bf16[128,256]{1,0:T(8,128)(2,1)} %self_weight.1, ...), custom_call_target="tpu_custom_call" | custom-call | tf_op jit(solution)/shard_map/graph_layer/pallas_call | solution.py:460
  50.2 1.8 %place_outputs.1 = (bf16[32,2048]{1,0:T(8,128)(2,1)}, bf16[16,2048]{1,0:T(8,128)(2,1)}, f32[128,256]{1,0:T(8,128)}, f32[128,256]{1,0:T(8,128)}, f32[1,256]{1,0:T(1,128)}) custom-call(bf16[32,2048]{1,0:T(8,128)(2,1)} %get-tuple-element.15.refs_0_, bf16[16,2048]{1,0:T(8,128)(2,1)} %get-tuple-element.16.refs_1_, f32[128,256]{1,0:T(8,128)} %get-tuple-element.17.refs_2_, ...), custom_call_target="tpu_custom_call" | custom-call | tf_op jit(solution)/shard_map/place_outputs/pallas_call | solution.py:533

commit v4 on v3

--- a/solution.py
+++ b/solution.py
@@ -33,6 +33,10 @@
 
 def dot_nn(a, b):
     return lax.dot_general(a, b, (((1,), (0,)), ((), ())), preferred_element_type=F32)
+
+
+def ring(step, size):
+    return min(step, size - step)
 
 
 def drain(ref, sem):
@@ -70,26 +74,24 @@
     cotangent,
     activated,
     grad_features,
-    grad_self,
-    grad_neigh,
+    grad_tiles,
     grad_bias,
     tile_rows,
     tile_cols,
     send_blocks,
     slots,
     gf,
-    gs,
-    gn,
     gb,
     fv,
     tiles,
     w_self,
     w_neigh,
-    w_cat,
-    w_t,
+    wt_self,
+    wt_neigh,
     bias_row,
     bias_mat,
     xg,
+    pre_self,
     ct,
     own_tab,
     tab,
@@ -112,7 +114,7 @@
     rs_recv,
     y_src,
     y_recv,
-    g_full,
+    g_half,
     b_full,
     local_sem,
     send_sem,
@@ -138,15 +140,15 @@
     my_x = lax.rem(q, X_SIZE)
 
     offsets = (1, 2, dom_size - 1, dom_size // 2)
-    y_peers = [lax.rem(fy + i, y_size) for i in range(1, y_size)]
+    y_steps = sorted(range(1, y_size), key=lambda d: -ring(d, y_size))
+    y_peers = [lax.rem(fy + d, y_size) for d in y_steps]
     sibling = (q * CORES + 1 - core, fy)
-    xz_peers = []
-    for dz in range(z_size):
-        for dx in range(X_SIZE):
-            if dz or dx:
-                pz = lax.rem(my_z + dz, z_size)
-                px = lax.rem(my_x + dx, X_SIZE)
-                xz_peers.append((dz, pz * X_SIZE + px))
+    xz_steps = [(dz, dx) for dz in range(z_size) for dx in range(X_SIZE) if dz or dx]
+    xz_steps.sort(key=lambda d: -ring(d[0], z_size) - ring(d[1], X_SIZE))
+    xz_peers = [
+        (dz, lax.rem(my_z + dz, z_size) * X_SIZE + lax.rem(my_x + dx, X_SIZE))
+        for dz, dx in xz_steps
+    ]
 
     def columns(ref, y):
         return ref.at[:, pl.ds(pl.multiple_of(y * vc, vc), vc)]
@@ -170,11 +172,11 @@
         copy.start()
 
     barrier = pltpu.get_barrier_semaphore()
-    greet = [(dom, p) for p in y_peers]
-    for off in (1, 2, dom_size - 1, dom_size - 2, dom_size // 2):
+    greet = [(p * CORES + core, fy) for _, p in xz_peers]
+    greet += [(dom, p) for p in y_peers]
+    for off in (dom_size // 2, 1, 2, dom_size - 1, dom_size - 2):
         greet.append((lax.rem(dom + off, dom_size), fy))
     greet.append(sibling)
-    greet += [(p * CORES + core, fy) for _, p in xz_peers]
     for device in greet:
         pl.semaphore_signal(barrier, inc=1, device_id=device, device_id_type=MESH)
 
@@ -192,7 +194,7 @@
 
     pl.semaphore_wait(barrier, len(greet))
 
-    for pos in range(4):
+    for pos in (3, 1, 0, 2):
         to = lax.rem(dom + offsets[pos], dom_size)
         remote(
             stage.at[pos],
@@ -202,12 +204,12 @@
             (to, fy),
         ).start()
     for p in y_peers:
-        remote(columns(fv, p), xg.at[fy, 0], send_sem.at[1], recv_sem.at[1], (dom, p)).start()
+        remote(columns(fv, p), xg.at[0, fy], send_sem.at[1], recv_sem.at[1], (dom, p)).start()
     for p in y_peers:
         remote(columns(cotangent, p), ct.at[fy], send_sem.at[2], recv_sem.at[2], (dom, p)).start()
     own_cot = pltpu.make_async_copy(columns(cotangent, fy), ct.at[fy], local_sem.at[8])
     own_cot.start()
-    xg[fy, 0] = fv[:, pl.ds(pl.multiple_of(fy * vc, vc), vc)]
+    xg[0, fy] = fv[:, pl.ds(pl.multiple_of(fy * vc, vc), vc)]
 
     for copy in loads[2:]:
         copy.wait()
@@ -241,32 +243,29 @@
     for b in range(nb):
         agg[b // vb, :, (b % vb) * BLOCK : (b % vb + 1) * BLOCK] = sums[b * fr : (b + 1) * fr]
     for p in y_peers:
-        remote(agg.at[p], xg.at[fy, 1], send_sem.at[3], recv_sem.at[3], (dom, p)).start()
-    xg[fy, 1] = agg[fy]
-
-    for y in range(y_size):
-        w_cat[y, 0] = w_self[y * fr : (y + 1) * fr, :]
-        w_cat[y, 1] = w_neigh[y * fr : (y + 1) * fr, :]
-    weights = w_cat[...].reshape(2 * in_dim, hidden)
-    w_t[...] = weights.astype(F32).T.astype(BF16)
+        remote(agg.at[p], xg.at[1, fy], send_sem.at[3], recv_sem.at[3], (dom, p)).start()
+    xg[1, fy] = agg[fy]
+
+    for src, dst in ((w_self, wt_self), (w_neigh, wt_neigh)):
+        dst[...] = src[...].astype(F32).T.astype(BF16)
     bias_mat[...] = jnp.broadcast_to(bias_row[...], (128, hidden)).T
     one_hot(slots, 16, fr, nb, by_far)
     one_hot(slots, nb, fr, 0, by_near)
 
+    drain(xg.at[0, 0:others], recv_sem.at[1])
+    early = dot_nn(wt_self[...], xg[0].reshape(in_dim, vc))
+    pre_self[...] = early + jnp.concatenate([bias_mat[...]] * vb, axis=1)
     own_cot.wait()
-    drain(xg.at[0:others, 0], recv_sem.at[1])
     drain(ct.at[0:others], recv_sem.at[2])
     drain(agg.at[0:others], recv_sem.at[3])
-
-    both = xg[...].reshape(2 * in_dim, vc)
-    pre = dot_nn(w_t[...], both) + jnp.concatenate([bias_mat[...]] * vb, axis=1)
+    pre = pre_self[...] + dot_nn(wt_neigh[...], xg[1].reshape(in_dim, vc))
     sigma = jax.nn.sigmoid(pre)
     cot = ct[...].reshape(hidden, vc).astype(F32)
     dpre = (cot * sigma * (1.0 + pre * (1.0 - sigma))).astype(BF16)
 
     bias_part = dot_nt(jnp.ones((16, vc), BF16), dpre)
     for kind, out in ((1 - core, part_send), (core, part_own)):
-        grads = dot_nt(xg[:, kind].reshape(in_dim, vc), dpre)
+        grads = dot_nt(xg[kind].reshape(in_dim, vc), dpre)
         half = jnp.where(kind == 0, bias_part[0:1, 0:128], bias_part[0:1, 128:256])
         for rt in range(row_tiles):
             for c in range(2):
@@ -279,7 +278,8 @@
         if out is part_send:
             swap = remote(part_send, part_recv, send_sem.at[4], recv_sem.at[4], sibling)
             swap.start()
-    bk[...] = dot_nn(weights, dpre).astype(BF16).reshape(y_size, 2 * fr, vc)
+    bk[:, 0:fr] = dot_nn(w_self[...], dpre).astype(BF16).reshape(y_size, fr, vc)
+    bk[:, fr : 2 * fr] = dot_nn(w_neigh[...], dpre).astype(BF16).reshape(y_size, fr, vc)
     for p in y_peers:
         remote(bk.at[p], bkr.at[fy], send_sem.at[5], recv_sem.at[5], (dom, p)).start()
     bkr[fy] = bk[fy]
@@ -306,7 +306,7 @@
     sums = dot_nn(by_far[...], high) + dot_nn(by_far[...], low)
     for n in range(16):
         rb_send[n // 4, n % 4] = sums[n * fr : (n + 1) * fr]
-    for pos in range(4):
+    for pos in (3, 1, 0, 2):
         to = lax.rem(dom + dom_size - offsets[pos], dom_size)
         remote(
             rb_send.at[pos], rb_recv.at[pos], send_sem.at[7], recv_sem.at[7], (to, fy)
@@ -334,12 +334,12 @@
     for n in range(1, y_size):
         total = total + y_recv[n]
     total = total * norm_scale
-    g_full[core, q] = total[: 8 * tpq]
+    g_half[q] = total[: 8 * tpq]
     b_full[core] = total[8 * tpq : 8 * tpq + 1]
     for dz, p in xz_peers:
         remote(
-            g_full.at[core, q],
-            g_full.at[core, q],
+            g_half.at[q],
+            g_half.at[q],
             send_sem.at[10],
             plane_sem.at[dz],
             (p * CORES + core, fy),
@@ -364,36 +364,30 @@
     stores = [pltpu.make_async_copy(gf, grad_features, local_sem.at[0])]
     stores[0].start()
 
-    for dz in range(z_size):
-        drain(g_full.at[0, 0 : X_SIZE - (dz == 0)], plane_sem.at[dz])
-        plane = pl.ds(lax.rem(my_z + z_size - dz, z_size) * X_SIZE, X_SIZE)
-        remote(
-            g_full.at[core, plane],
-            g_full.at[core, plane],
-            send_sem.at[12],
-            recv_sem.at[11],
-            sibling,
-        ).start()
     bias_swap.wait_recv()
     for kind in range(2):
         gb[:, kind * 128 : (kind + 1) * 128] = b_full[kind]
     stores.append(pltpu.make_async_copy(gb, grad_bias, local_sem.at[1]))
     stores[1].start()
-    drain(g_full.at[0], recv_sem.at[11])
-    for kind, out, dst in ((0, gs, grad_self), (1, gn, grad_neigh)):
-        for rt in range(row_tiles):
-            for c in range(2):
-                n = rt * 2 + c
-                out[rt * 8 : (rt + 1) * 8, c * 128 : (c + 1) * 128] = g_full[
-                    kind, n // tpq, (n % tpq) * 8 : (n % tpq + 1) * 8, :
-                ]
-        stores.append(pltpu.make_async_copy(out, dst, local_sem.at[2 + kind]))
-        stores[-1].start()
+
+    for dz in sorted(range(z_size), key=lambda d: ring(d, z_size)):
+        drain(g_half.at[0 : X_SIZE - (dz == 0)], plane_sem.at[dz])
+        plane = pl.ds(lax.rem(my_z + z_size - dz, z_size) * X_SIZE, X_SIZE)
+        remote(
+            g_half.at[plane],
+            grad_tiles.at[core, plane],
+            send_sem.at[12],
+            recv_sem.at[11],
+            sibling,
+        ).start()
+    stores.append(pltpu.make_async_copy(g_half, grad_tiles.at[core], local_sem.at[2]))
+    stores[2].start()
     own_act.wait()
     drain(activated.at[:, 0 : others * vc], recv_sem.at[9])
+    drain(g_half, recv_sem.at[11])
 
     drain(stage, send_sem.at[0])
-    drain(xg.at[0:others, 0], send_sem.at[1])
+    drain(xg.at[0, 0:others], send_sem.at[1])
     drain(ct.at[0:others], send_sem.at[2])
     drain(agg.at[0:others], send_sem.at[3])
     swap.wait_send()
@@ -402,24 +396,33 @@
     drain(rb_recv, send_sem.at[7])
     drain(y_recv.at[0:others], send_sem.at[8])
     drain(activated.at[:, 0 : others * vc], send_sem.at[9])
-    drain(g_full.at[0, 0 : xz - 1], send_sem.at[10])
+    drain(g_half.at[0 : xz - 1], send_sem.at[10])
     bias_swap.wait_send()
-    drain(g_full.at[0], send_sem.at[12])
+    drain(g_half, send_sem.at[12])
     for copy in stores:
         copy.wait()
 
 
 def place(*refs):
-    count = len(refs) // 3
-    sems = refs[-1]
-    ins, outs, held = refs[:count], refs[count : 2 * count], refs[2 * count : 3 * count]
-    first = [pltpu.make_async_copy(ins[i], held[i], sems.at[0, i]) for i in range(count)]
-    second = [pltpu.make_async_copy(held[i], outs[i], sems.at[1, i]) for i in range(count)]
+    ins, outs, held, (gs, gn, sems) = refs[0:4], refs[4:9], refs[9:13], refs[13:16]
+    first = [pltpu.make_async_copy(ins[i], held[i], sems.at[0, i]) for i in range(4)]
+    ready = (held[0], held[1], gs, gn, held[3])
+    second = [pltpu.make_async_copy(ready[i], outs[i], sems.at[1, i]) for i in range(5)]
     for copy in first:
         copy.start()
-    for a, b in zip(first, second):
-        a.wait()
-        b.start()
+    first[2].wait()
+    tiles = held[2]
+    rows = tiles.shape[2]
+    for kind, out in ((0, gs), (1, gn)):
+        for n in range(2 * out.shape[0] // 8):
+            rt, c, part = n // 2, n % 2, (n % (rows // 8)) * 8
+            out[rt * 8 : (rt + 1) * 8, c * 128 : (c + 1) * 128] = tiles[
+                kind, n // (rows // 8), part : part + 8, :
+            ]
+        second[2 + kind].start()
+    for i, o in ((0, 0), (1, 1), (3, 4)):
+        first[i].wait()
+        second[o].start()
     for copy in second:
         copy.wait()
 
@@ -462,30 +465,28 @@
         out_shape=(
             jax.ShapeDtypeStruct((hr, vertices), BF16),
             jax.ShapeDtypeStruct((fr, vertices), BF16),
-            jax.ShapeDtypeStruct((in_dim, hidden), F32),
-            jax.ShapeDtypeStruct((in_dim, hidden), F32),
+            jax.ShapeDtypeStruct((2, xz, 8 * tpq, 128), F32),
             jax.ShapeDtypeStruct((1, hidden), F32),
         ),
         in_specs=[hbm] * 9,
-        out_specs=(hbm,) * 5,
+        out_specs=(hbm,) * 4,
         scratch_shapes=[
             pltpu.SMEM((tile_count,), jnp.int32),
             pltpu.SMEM((tile_count,), jnp.int32),
             pltpu.SMEM((1, 4, dom_size), jnp.int32),
             pltpu.SMEM((tile_count,), jnp.int32),
             pltpu.VMEM((fr, vertices), BF16),
-            pltpu.VMEM((in_dim, hidden), F32),
-            pltpu.VMEM((in_dim, hidden), F32),
             pltpu.VMEM((1, hidden), F32),
             pltpu.VMEM((fr, vertices), BF16),
             pltpu.VMEM((tile_count, BLOCK, BLOCK), BF16),
             pltpu.VMEM((in_dim, hidden), BF16),
             pltpu.VMEM((in_dim, hidden), BF16),
-            pltpu.VMEM((y_size, 2, fr, hidden), BF16),
-            pltpu.VMEM((hidden, 2 * in_dim), BF16),
+            pltpu.VMEM((hidden, in_dim), BF16),
+            pltpu.VMEM((hidden, in_dim), BF16),
             pltpu.VMEM((1, hidden), F32),
             pltpu.VMEM((hidden, 128), F32),
-            pltpu.VMEM((y_size, 2, fr, vc), BF16),
+            pltpu.VMEM((2, y_size, fr, vc), BF16),
+            pltpu.VMEM((hidden, vc), F32),
             pltpu.VMEM((y_size, hr, vc), BF16),
             pltpu.VMEM((nb, fr, BLOCK), BF16),
             pltpu.VMEM((nb + 16, fr, BLOCK), BF16),
@@ -508,7 +509,7 @@
             pltpu.VMEM((xz, ext, 128), F32),
             pltpu.VMEM((ext, 128), F32),
             pltpu.VMEM((y_size, ext, 128), F32),
-            pltpu.VMEM((2, xz, 8 * tpq, 128), F32),
+            pltpu.VMEM((xz, 8 * tpq, 128), F32),
             pltpu.VMEM((2, 1, 128), F32),
             dma((10,)),
             dma((13,)),
@@ -530,12 +531,21 @@
         tile_values,
         cotangent,
     )
+    weight = jax.ShapeDtypeStruct((in_dim, hidden), F32)
     outs = pl.pallas_call(
         place,
-        out_shape=tuple(jax.ShapeDtypeStruct(o.shape, o.dtype) for o in outs),
-        in_specs=[hbm] * 5,
+        out_shape=(
+            jax.ShapeDtypeStruct((hr, vertices), BF16),
+            jax.ShapeDtypeStruct((fr, vertices), BF16),
+            weight,
+            weight,
+            jax.ShapeDtypeStruct((1, hidden), F32),
+        ),
+        in_specs=[hbm] * 4,
         out_specs=(hbm,) * 5,
-        scratch_shapes=[pltpu.VMEM(o.shape, o.dtype) for o in outs] + [dma((2, 5))],
+        scratch_shapes=[pltpu.VMEM(o.shape, o.dtype) for o in outs]
+        + [pltpu.VMEM((in_dim, hidden), F32)] * 2
+        + [dma((2, 5))],
         compiler_params=pltpu.CompilerParams(vmem_limit_bytes=56 * 1024 * 1024),
         name="place_outputs",
     )(*outs)

time: 52.1 us -> 49.9 us (0.958)
  Pallas kernels: 51.3 us -> 49.1 us
    pallas_call x1, Pallas kernels: 49.5 us -> 47.2 us  [local(): pl.pallas_call(functools.partial(kernel, dims), out_shape=(jax.ShapeDtype...]
where the time goes in v4:
time: 49.9 us; the launch traced here: 49.7 us
  Pallas kernels  49.1 us (98%)
  between operations  0.64 us (1%)
    pallas_call x1, Pallas kernels, local(): pl.pallas_call(functools.partial(kernel, dims), out_shape=(jax.ShapeDtype...  47.2 us
    pallas_call x1, Pallas kernels, local(): pl.pallas_call(place, out_shape=(jax.ShapeDtypeStruct((hr, vertices), BF1...  1.91 us

profile of v4, /device:TPU:1, one launch (start us, length us, event | category | flops | bytes accessed | tf_op | source)
XLA Modules:
  0.0 49.7 jit_solution(8469426027009608003)
XLA Ops:
  0.6 47.2 %graph_layer.1 = (bf16[32,2048]{1,0:T(8,128)(2,1)}, bf16[16,2048]{1,0:T(8,128)(2,1)}, f32[2,32,8,128]{3,2,1,0:T(8,128)}, f32[1,256]{1,0:T(1,128)}) custom-call(s32[64]{0:T(128)} %rows_in.1, s32[64]{0:T(128)} %cols_in.1, s32[1,4,64]{2,1,0:T(4,128)} %bitcast.3, bf16[16,2048]{1,0:T(8,128)(2,1)} %features.1, bf16[128,256]{1,0:T(8,128)(2,1)} %self_weight.1, ...), custom_call_target="tpu_custom_call" | custom-call | tf_op jit(solution)/shard_map/graph_layer/pallas_call | solution.py:463
  47.8 1.9 %place_outputs.1 = (bf16[32,2048]{1,0:T(8,128)(2,1)}, bf16[16,2048]{1,0:T(8,128)(2,1)}, f32[128,256]{1,0:T(8,128)}, f32[128,256]{1,0:T(8,128)}, f32[1,256]{1,0:T(1,128)}) custom-call(bf16[32,2048]{1,0:T(8,128)(2,1)} %get-tuple-element.14.refs_0_, bf16[16,2048]{1,0:T(8,128)(2,1)} %get-tuple-element.15.refs_1_, f32[2,32,8,128]{3,2,1,0:T(8,128)} %get-tuple-element.16.refs_2_, ...), custom_call_target="tpu_custom_call" | custom-call | tf_op jit(solution)/shard_map/place_outputs/pallas_call | solution.py:535

commit v5 on v4

--- a/solution.py
+++ b/solution.py
@@ -58,7 +58,12 @@
 
 def split(value):
     high = value.astype(BF16)
-    return high, (value - high.astype(F32)).astype(BF16)
+    return jnp.concatenate([high, (value - high.astype(F32)).astype(BF16)], axis=1)
+
+
+def added(one_hots, parts):
+    both = dot_nn(one_hots[...], parts[...].reshape(one_hots.shape[1], 2 * BLOCK))
+    return both[:, :BLOCK] + both[:, BLOCK:]
 
 
 def kernel(
@@ -116,6 +121,7 @@
     y_recv,
     g_half,
     b_full,
+    z_sem,
     local_sem,
     send_sem,
     recv_sem,
@@ -168,17 +174,21 @@
             )
         )
     ]
-    for copy in loads:
-        copy.start()
-
     barrier = pltpu.get_barrier_semaphore()
-    greet = [(p * CORES + core, fy) for _, p in xz_peers]
-    greet += [(dom, p) for p in y_peers]
-    for off in (dom_size // 2, 1, 2, dom_size - 1, dom_size - 2):
+    z_peers = [
+        ((lax.rem(my_z + d, z_size) * X_SIZE + my_x) * CORES + core, fy)
+        for d in sorted(range(1, z_size), key=lambda d: -ring(d, z_size))
+    ]
+    greet = z_peers + [(dom, p) for p in y_peers]
+    for off in (1, dom_size - 1, 2, dom_size - 2):
         greet.append((lax.rem(dom + off, dom_size), fy))
+    for d in range(1, X_SIZE):
+        greet.append(((my_z * X_SIZE + lax.rem(my_x + d, X_SIZE)) * CORES + core, fy))
     greet.append(sibling)
     for device in greet:
         pl.semaphore_signal(barrier, inc=1, device_id=device, device_id_type=MESH)
+    for copy in loads:
+        copy.start()
 
     loads[0].wait()
     owners = []
@@ -209,6 +219,8 @@
         remote(columns(cotangent, p), ct.at[fy], send_sem.at[2], recv_sem.at[2], (dom, p)).start()
     own_cot = pltpu.make_async_copy(columns(cotangent, fy), ct.at[fy], local_sem.at[8])
     own_cot.start()
+    for device in z_peers:
+        pl.semaphore_signal(z_sem, inc=1, device_id=device, device_id_type=MESH)
     xg[0, fy] = fv[:, pl.ds(pl.multiple_of(fy * vc, vc), vc)]
 
     for copy in loads[2:]:
@@ -234,12 +246,11 @@
     drain(stage, recv_sem.at[0])
 
     def agg_body(t, carry):
-        prod[t] = dot_nt(tab[slots[t]], tiles[t])
+        prod[t] = split(dot_nt(tab[slots[t]], tiles[t]))
         return carry
 
     lax.fori_loop(0, tile_count, agg_body, 0, unroll=tile_count)
-    high, low = split(prod[...].reshape(tile_count * fr, BLOCK))
-    sums = (dot_nn(by_row[...], high) + dot_nn(by_row[...], low)).astype(BF16)
+    sums = added(by_row, prod).astype(BF16)
     for b in range(nb):
         agg[b // vb, :, (b % vb) * BLOCK : (b % vb + 1) * BLOCK] = sums[b * fr : (b + 1) * fr]
     for p in y_peers:
@@ -286,6 +297,7 @@
     act[...] = (pre * sigma).astype(BF16).reshape(y_size, hr, vc)
 
     swap.wait_recv()
+    pl.semaphore_wait(z_sem, z_size - 1)
     rs_src[...] = part_own[...] + part_recv[...]
     for _, p in xz_peers:
         remote(
@@ -298,12 +310,11 @@
         btab[b] = bkr[b // vb, fr : 2 * fr, (b % vb) * BLOCK : (b % vb + 1) * BLOCK]
 
     def spread_body(t, carry):
-        prod[t] = dot_nn(btab[tile_rows[t]], tiles[t])
+        prod[t] = split(dot_nn(btab[tile_rows[t]], tiles[t]))
         return carry
 
     lax.fori_loop(0, tile_count, spread_body, 0, unroll=tile_count)
-    high, low = split(prod[...].reshape(tile_count * fr, BLOCK))
-    sums = dot_nn(by_far[...], high) + dot_nn(by_far[...], low)
+    sums = added(by_far, prod)
     for n in range(16):
         rb_send[n // 4, n % 4] = sums[n * fr : (n + 1) * fr]
     for pos in (3, 1, 0, 2):
@@ -327,7 +338,7 @@
     own_act = pltpu.make_async_copy(act.at[fy], columns(activated, fy), local_sem.at[9])
     own_act.start()
 
-    near = dot_nn(by_near[...], high) + dot_nn(by_near[...], low)
+    near = added(by_near, prod)
 
     drain(y_recv.at[0:others], recv_sem.at[8])
     total = y_recv[0]
@@ -496,7 +507,7 @@
             pltpu.VMEM((y_size, 2 * fr, vc), BF16),
             pltpu.VMEM((y_size, 2 * fr, vc), BF16),
             pltpu.VMEM((nb, fr, BLOCK), BF16),
-            pltpu.VMEM((tile_count, fr, BLOCK), F32),
+            pltpu.VMEM((tile_count, fr, 2 * BLOCK), BF16),
             pltpu.VMEM((nb * fr, tile_count * fr), BF16),
             pltpu.VMEM((16 * fr, tile_count * fr), BF16),
             pltpu.VMEM((nb * fr, tile_count * fr), BF16),
@@ -511,6 +522,7 @@
             pltpu.VMEM((y_size, ext, 128), F32),
             pltpu.VMEM((xz, 8 * tpq, 128), F32),
             pltpu.VMEM((2, 1, 128), F32),
+            pltpu.SemaphoreType.REGULAR,
             dma((10,)),
             dma((13,)),
             dma((12,)),

time: 49.9 us -> 49.8 us (level)
  no operation moved by 1% of the time
where the time goes in v5:
time: 49.8 us; the launch traced here: 49.6 us
  Pallas kernels  49 us (98%)
  between operations  0.64 us (1%)
    pallas_call x1, Pallas kernels, local(): pl.pallas_call(functools.partial(kernel, dims), out_shape=(jax.ShapeDtype...  47 us
    pallas_call x1, Pallas kernels, local(): pl.pallas_call(place, out_shape=(jax.ShapeDtypeStruct((hr, vertices), BF1...  1.91 us

profile of v5, /device:TPU:1, one launch (start us, length us, event | category | flops | bytes accessed | tf_op | source)
XLA Modules:
  0.0 49.6 jit_solution(8752161830357760166)
XLA Ops:
  0.6 47.0 %graph_layer.1 = (bf16[32,2048]{1,0:T(8,128)(2,1)}, bf16[16,2048]{1,0:T(8,128)(2,1)}, f32[2,32,8,128]{3,2,1,0:T(8,128)}, f32[1,256]{1,0:T(1,128)}) custom-call(s32[64]{0:T(128)} %rows_in.1, s32[64]{0:T(128)} %cols_in.1, s32[1,4,64]{2,1,0:T(4,128)} %bitcast.3, bf16[16,2048]{1,0:T(8,128)(2,1)} %features.1, bf16[128,256]{1,0:T(8,128)(2,1)} %self_weight.1, ...), custom_call_target="tpu_custom_call" | custom-call | tf_op jit(solution)/shard_map/graph_layer/pallas_call | solution.py:474
  47.7 1.9 %place_outputs.1 = (bf16[32,2048]{1,0:T(8,128)(2,1)}, bf16[16,2048]{1,0:T(8,128)(2,1)}, f32[128,256]{1,0:T(8,128)}, f32[128,256]{1,0:T(8,128)}, f32[1,256]{1,0:T(1,128)}) custom-call(bf16[32,2048]{1,0:T(8,128)(2,1)} %get-tuple-element.14.refs_0_, bf16[16,2048]{1,0:T(8,128)(2,1)} %get-tuple-element.15.refs_1_, f32[2,32,8,128]{3,2,1,0:T(8,128)} %get-tuple-element.16.refs_2_, ...), custom_call_target="tpu_custom_call" | custom-call | tf_op jit(solution)/shard_map/place_outputs/pallas_call | solution.py:547

commit v6 on v5

--- a/solution.py
+++ b/solution.py
@@ -415,14 +415,12 @@
 
 
 def place(*refs):
-    ins, outs, held, (gs, gn, sems) = refs[0:4], refs[4:9], refs[9:13], refs[13:16]
-    first = [pltpu.make_async_copy(ins[i], held[i], sems.at[0, i]) for i in range(4)]
-    ready = (held[0], held[1], gs, gn, held[3])
-    second = [pltpu.make_async_copy(ready[i], outs[i], sems.at[1, i]) for i in range(5)]
-    for copy in first:
-        copy.start()
-    first[2].wait()
-    tiles = held[2]
+    ins, outs, (gs, gn, sems) = refs[0:4], refs[4:9], refs[9:12]
+    tiles = ins[2]
+    ready = (ins[0], ins[1], gs, gn, ins[3])
+    copies = [pltpu.make_async_copy(ready[i], outs[i], sems.at[i]) for i in range(5)]
+    for i in (0, 1, 4):
+        copies[i].start()
     rows = tiles.shape[2]
     for kind, out in ((0, gs), (1, gn)):
         for n in range(2 * out.shape[0] // 8):
@@ -430,11 +428,8 @@
             out[rt * 8 : (rt + 1) * 8, c * 128 : (c + 1) * 128] = tiles[
                 kind, n // (rows // 8), part : part + 8, :
             ]
-        second[2 + kind].start()
-    for i, o in ((0, 0), (1, 1), (3, 4)):
-        first[i].wait()
-        second[o].start()
-    for copy in second:
+        copies[2 + kind].start()
+    for copy in copies:
         copy.wait()
 
 
@@ -529,19 +524,24 @@
             dma((xz // X_SIZE,)),
         ],
         compiler_params=pltpu.CompilerParams(
-            collective_id=0, has_side_effects=True, vmem_limit_bytes=56 * 1024 * 1024
+            collective_id=0, has_side_effects=True, vmem_limit_bytes=24 * 1024 * 1024
         ),
         name="graph_layer",
     )(
-        tile_rows,
-        tile_cols,
-        send_blocks.transpose(0, 2, 1),
-        features,
-        self_weight,
-        neigh_weight,
-        bias_vector.reshape(1, hidden),
-        tile_values,
-        cotangent,
+        *[
+            pltpu.with_memory_space_constraint(operand, pltpu.HBM)
+            for operand in (
+                tile_rows,
+                tile_cols,
+                send_blocks.transpose(0, 2, 1),
+                features,
+                self_weight,
+                neigh_weight,
+                bias_vector.reshape(1, hidden),
+                tile_values,
+                cotangent,
+            )
+        ]
     )
     weight = jax.ShapeDtypeStruct((in_dim, hidden), F32)
     outs = pl.pallas_call(
@@ -553,12 +553,14 @@
             weight,
             jax.ShapeDtypeStruct((1, hidden), F32),
         ),
-        in_specs=[hbm] * 4,
+        in_specs=[hbm, hbm, pl.BlockSpec(memory_space=pltpu.VMEM), hbm],
         out_specs=(hbm,) * 5,
-        scratch_shapes=[pltpu.VMEM(o.shape, o.dtype) for o in outs]
-        + [pltpu.VMEM((in_dim, hidden), F32)] * 2
-        + [dma((2, 5))],
-        compiler_params=pltpu.CompilerParams(vmem_limit_bytes=56 * 1024 * 1024),
+        scratch_shapes=[
+            pltpu.VMEM((in_dim, hidden), F32),
+            pltpu.VMEM((in_dim, hidden), F32),
+            dma((5,)),
+        ],
+        compiler_params=pltpu.CompilerParams(vmem_limit_bytes=8 * 1024 * 1024),
         name="place_outputs",
     )(*outs)
     activated, grad_features, grad_self, grad_neigh, grad_bias = outs

time: 49.8 us -> 48.5 us (0.974)
  Pallas kernels: 49 us -> 47.7 us
    pallas_call x1, Pallas kernels: 1.91 us -> 0.82 us  [local(): pl.pallas_call(place, out_shape=(jax.ShapeDtypeStruct((hr, vertices), BF1...]
where the time goes in v6:
time: 48.5 us; the launch traced here: 48.3 us
  Pallas kernels  47.7 us (98%)
  between operations  0.64 us (1%)
    pallas_call x1, Pallas kernels, local(): pl.pallas_call(functools.partial(kernel, dims), out_shape=(jax.ShapeDtype...  46.9 us

profile of v6, /device:TPU:1, one launch (start us, length us, event | category | flops | bytes accessed | tf_op | source)
XLA Modules:
  0.0 48.3 jit_solution(10673600793594292505)
XLA Ops:
  0.6 46.9 %graph_layer.1 = (bf16[32,2048]{1,0:T(8,128)(2,1)S(1)}, bf16[16,2048]{1,0:T(8,128)(2,1)S(1)}, f32[2,32,8,128]{3,2,1,0:T(8,128)S(1)}, f32[1,256]{1,0:T(1,128)S(1)}) custom-call(s32[64]{0:T(128)} %rows_in.1, s32[64]{0:T(128)} %cols_in.1, s32[1,4,64]{2,1,0:T(4,128)} %bitcast.3, bf16[16,2048]{1,0:T(8,128)(2,1)} %features.1, bf16[128,256]{1,0:T(8,128)(2,1)} %self_weight.1, ...), custom_call_target="tpu_custom_call" | custom-call | tf_op jit(solution)/shard_map/graph_layer/pallas_call | solution.py:469
  47.5 0.8 %place_outputs.1 = (bf16[32,2048]{1,0:T(8,128)(2,1)}, bf16[16,2048]{1,0:T(8,128)(2,1)}, f32[128,256]{1,0:T(8,128)}, f32[128,256]{1,0:T(8,128)}, f32[1,256]{1,0:T(1,128)}) custom-call(bf16[32,2048]{1,0:T(8,128)(2,1)S(1)} %get-tuple-element.14.refs_0_, bf16[16,2048]{1,0:T(8,128)(2,1)S(1)} %get-tuple-element.15.refs_1_, ...), custom_call_target="tpu_custom_call" | custom-call | tf_op jit(solution)/shard_map/place_outputs/pallas_call | solution.py:547

commit v7 on v6

--- a/solution.py
+++ b/solution.py
@@ -112,20 +112,22 @@
     by_near,
     rb_send,
     rb_recv,
-    part_own,
-    part_send,
-    part_recv,
-    rs_src,
+    part,
     rs_recv,
+    t_src,
+    t_core,
     y_src,
     y_recv,
-    g_half,
-    b_full,
+    g_src,
+    b_src,
+    b_core,
+    b_y,
+    b_z,
+    b_x,
     z_sem,
     local_sem,
     send_sem,
     recv_sem,
-    plane_sem,
 ):
     dom_size, y_size, nb, tile_count, in_dim, hidden, norm_scale = dims
     z_size = dom_size // (X_SIZE * CORES)
@@ -134,8 +136,8 @@
     hr = hidden // y_size
     vb = nb // y_size
     vc = vb * BLOCK
-    tpq = (in_dim // 8) * (hidden // 128) // xz
-    row_tiles = in_dim // 8
+    col_tiles = hidden // 128
+    tpq = (2 * in_dim // 16) * col_tiles // xz
     others = y_size - 1
 
     dom = lax.axis_index("dom")
@@ -152,7 +154,7 @@
     xz_steps = [(dz, dx) for dz in range(z_size) for dx in range(X_SIZE) if dz or dx]
     xz_steps.sort(key=lambda d: -ring(d[0], z_size) - ring(d[1], X_SIZE))
     xz_peers = [
-        (dz, lax.rem(my_z + dz, z_size) * X_SIZE + lax.rem(my_x + dx, X_SIZE))
+        lax.rem(my_z + dz, z_size) * X_SIZE + lax.rem(my_x + dx, X_SIZE)
         for dz, dx in xz_steps
     ]
 
@@ -182,8 +184,10 @@
     greet = z_peers + [(dom, p) for p in y_peers]
     for off in (1, dom_size - 1, 2, dom_size - 2):
         greet.append((lax.rem(dom + off, dom_size), fy))
-    for d in range(1, X_SIZE):
-        greet.append(((my_z * X_SIZE + lax.rem(my_x + d, X_SIZE)) * CORES + core, fy))
+    x_peers = [
+        ((my_z * X_SIZE + lax.rem(my_x + d, X_SIZE)) * CORES + core, fy) for d in range(1, X_SIZE)
+    ]
+    greet += x_peers
     greet.append(sibling)
     for device in greet:
         pl.semaphore_signal(barrier, inc=1, device_id=device, device_id_type=MESH)
@@ -274,21 +278,23 @@
     cot = ct[...].reshape(hidden, vc).astype(F32)
     dpre = (cot * sigma * (1.0 + pre * (1.0 - sigma))).astype(BF16)
 
-    bias_part = dot_nt(jnp.ones((16, vc), BF16), dpre)
-    for kind, out in ((1 - core, part_send), (core, part_own)):
-        grads = dot_nt(xg[kind].reshape(in_dim, vc), dpre)
-        half = jnp.where(kind == 0, bias_part[0:1, 0:128], bias_part[0:1, 128:256])
-        for rt in range(row_tiles):
-            for c in range(2):
-                n = rt * 2 + c
-                out[n // tpq, (n % tpq) * 8 : (n % tpq + 1) * 8, :] = grads[
-                    rt * 8 : (rt + 1) * 8, c * 128 : (c + 1) * 128
-                ]
-        for n in range(xz):
-            out[n, 8 * tpq : 8 * tpq + 1, :] = half
-        if out is part_send:
-            swap = remote(part_send, part_recv, send_sem.at[4], recv_sem.at[4], sibling)
-            swap.start()
+    b_src[0] = dot_nt(jnp.ones((16, vc), BF16), dpre)[0:1]
+    bias_swap = remote(b_src.at[0], b_core, send_sem.at[4], recv_sem.at[4], sibling)
+    bias_swap.start()
+    grads = dot_nt(xg[...].reshape(2 * in_dim, vc), dpre).astype(BF16)
+    for rt in range(2 * in_dim // 16):
+        for c in range(col_tiles):
+            n = rt * col_tiles + c
+            part[n // tpq, (n % tpq) * 16 : (n % tpq + 1) * 16, :] = grads[
+                rt * 16 : (rt + 1) * 16, c * 128 : (c + 1) * 128
+            ]
+    pl.semaphore_wait(z_sem, z_size - 1)
+    for p in xz_peers:
+        remote(
+            part.at[p], rs_recv.at[q], send_sem.at[6], recv_sem.at[6], (p * CORES + core, fy)
+        ).start()
+    rs_recv[q] = part[q]
+
     bk[:, 0:fr] = dot_nn(w_self[...], dpre).astype(BF16).reshape(y_size, fr, vc)
     bk[:, fr : 2 * fr] = dot_nn(w_neigh[...], dpre).astype(BF16).reshape(y_size, fr, vc)
     for p in y_peers:
@@ -296,14 +302,40 @@
     bkr[fy] = bk[fy]
     act[...] = (pre * sigma).astype(BF16).reshape(y_size, hr, vc)
 
+    bias_swap.wait_recv()
+    b_sum = b_src[0] + b_core[...]
+    b_src[1] = b_sum
+    b_y[fy] = b_sum
+    for p in y_peers:
+        remote(b_src.at[1], b_y.at[fy], send_sem.at[10], recv_sem.at[10], (dom, p)).start()
+
+    drain(rs_recv.at[0 : xz - 1], recv_sem.at[6])
+    total = rs_recv[0].astype(F32)
+    for n in range(1, xz):
+        total = total + rs_recv[n].astype(F32)
+    t_src[...] = total
+    swap = remote(t_src, t_core, send_sem.at[12], recv_sem.at[12], sibling)
+    swap.start()
+    drain(b_y.at[0:others], recv_sem.at[10])
+    b_sum = b_y[0]
+    for n in range(1, y_size):
+        b_sum = b_sum + b_y[n]
+    b_src[2] = b_sum
+    b_z[my_z] = b_sum
+    for device in z_peers:
+        remote(b_src.at[2], b_z.at[my_z], send_sem.at[11], recv_sem.at[11], device).start()
     swap.wait_recv()
-    pl.semaphore_wait(z_sem, z_size - 1)
-    rs_src[...] = part_own[...] + part_recv[...]
-    for _, p in xz_peers:
+    total = total + t_core[...]
+    y_src[...] = total
+    y_recv[fy] = total
+    for p in y_peers:
+        remote(y_src, y_recv.at[fy], send_sem.at[8], recv_sem.at[8], (dom, p)).start()
+    for p in y_peers:
         remote(
-            rs_src.at[p], rs_recv.at[q], send_sem.at[6], recv_sem.at[6], (p * CORES + core, fy)
+            act.at[p], columns(activated, fy), send_sem.at[9], recv_sem.at[9], (dom, p)
         ).start()
-    rs_recv[q] = rs_src[q]
+    own_act = pltpu.make_async_copy(act.at[fy], columns(activated, fy), local_sem.at[9])
+    own_act.start()
 
     drain(bkr.at[0:others], recv_sem.at[5])
     for b in range(nb):
@@ -323,42 +355,26 @@
             rb_send.at[pos], rb_recv.at[pos], send_sem.at[7], recv_sem.at[7], (to, fy)
         ).start()
 
-    drain(rs_recv.at[0 : xz - 1], recv_sem.at[6])
-    total = rs_recv[0]
-    for n in range(1, xz):
-        total = total + rs_recv[n]
-    y_src[...] = total
-    y_recv[fy] = total
-    for p in y_peers:
-        remote(y_src, y_recv.at[fy], send_sem.at[8], recv_sem.at[8], (dom, p)).start()
-    for p in y_peers:
-        remote(
-            act.at[p], columns(activated, fy), send_sem.at[9], recv_sem.at[9], (dom, p)
-        ).start()
-    own_act = pltpu.make_async_copy(act.at[fy], columns(activated, fy), local_sem.at[9])
-    own_act.start()
-
     near = added(by_near, prod)
 
     drain(y_recv.at[0:others], recv_sem.at[8])
     total = y_recv[0]
     for n in range(1, y_size):
         total = total + y_recv[n]
-    total = total * norm_scale
-    g_half[q] = total[: 8 * tpq]
-    b_full[core] = total[8 * tpq : 8 * tpq + 1]
-    for dz, p in xz_peers:
+    g_src[...] = (total * norm_scale).astype(BF16)
+    for p in xz_peers:
         remote(
-            g_half.at[q],
-            g_half.at[q],
-            send_sem.at[10],
-            plane_sem.at[dz],
-            (p * CORES + core, fy),
+            g_src, grad_tiles.at[q], send_sem.at[13], recv_sem.at[13], (p * CORES + core, fy)
         ).start()
-    bias_swap = remote(
-        b_full.at[core], b_full.at[core], send_sem.at[11], recv_sem.at[9 + 1], sibling
-    )
-    bias_swap.start()
+    stores = [pltpu.make_async_copy(g_src, grad_tiles.at[q], local_sem.at[2])]
+    drain(b_z.at[0 : z_size - 1], recv_sem.at[11])
+    b_sum = b_z[0]
+    for n in range(1, z_size):
+        b_sum = b_sum + b_z[n]
+    b_src[3] = b_sum
+    b_x[my_x] = b_sum
+    for device in x_peers:
+        remote(b_src.at[3], b_x.at[my_x], send_sem.at[14], recv_sem.at[14], device).start()
 
     drain(rb_recv, recv_sem.at[7])
     sums = [
@@ -372,44 +388,36 @@
             sums = [jnp.where(owners[pos][c] == b, v + term, v) for b, v in enumerate(sums)]
     for b in range(nb):
         gf[:, b * BLOCK : (b + 1) * BLOCK] = sums[b].astype(BF16)
-    stores = [pltpu.make_async_copy(gf, grad_features, local_sem.at[0])]
-    stores[0].start()
-
-    bias_swap.wait_recv()
-    for kind in range(2):
-        gb[:, kind * 128 : (kind + 1) * 128] = b_full[kind]
+    stores.append(pltpu.make_async_copy(gf, grad_features, local_sem.at[0]))
+    for copy in stores:
+        copy.start()
+
+    drain(b_x.at[0 : X_SIZE - 1], recv_sem.at[14])
+    b_sum = b_x[0]
+    for n in range(1, X_SIZE):
+        b_sum = b_sum + b_x[n]
+    gb[...] = b_sum * norm_scale
     stores.append(pltpu.make_async_copy(gb, grad_bias, local_sem.at[1]))
-    stores[1].start()
-
-    for dz in sorted(range(z_size), key=lambda d: ring(d, z_size)):
-        drain(g_half.at[0 : X_SIZE - (dz == 0)], plane_sem.at[dz])
-        plane = pl.ds(lax.rem(my_z + z_size - dz, z_size) * X_SIZE, X_SIZE)
-        remote(
-            g_half.at[plane],
-            grad_tiles.at[core, plane],
-            send_sem.at[12],
-            recv_sem.at[11],
-            sibling,
-        ).start()
-    stores.append(pltpu.make_async_copy(g_half, grad_tiles.at[core], local_sem.at[2]))
-    stores[2].start()
+    stores[-1].start()
     own_act.wait()
     drain(activated.at[:, 0 : others * vc], recv_sem.at[9])
-    drain(g_half, recv_sem.at[11])
+    drain(grad_tiles.at[0 : xz - 1], recv_sem.at[13])
 
     drain(stage, send_sem.at[0])
     drain(xg.at[0, 0:others], send_sem.at[1])
     drain(ct.at[0:others], send_sem.at[2])
     drain(agg.at[0:others], send_sem.at[3])
-    swap.wait_send()
+    bias_swap.wait_send()
     drain(bkr.at[0:others], send_sem.at[5])
     drain(rs_recv.at[0 : xz - 1], send_sem.at[6])
     drain(rb_recv, send_sem.at[7])
     drain(y_recv.at[0:others], send_sem.at[8])
     drain(activated.at[:, 0 : others * vc], send_sem.at[9])
-    drain(g_half.at[0 : xz - 1], send_sem.at[10])
-    bias_swap.wait_send()
-    drain(g_half, send_sem.at[12])
+    drain(b_y.at[0:others], send_sem.at[10])
+    drain(b_z.at[0 : z_size - 1], send_sem.at[11])
+    swap.wait_send()
+    drain(rs_recv.at[0 : xz - 1], send_sem.at[13])
+    drain(b_x.at[0 : X_SIZE - 1], send_sem.at[14])
     for copy in stores:
         copy.wait()
 
@@ -421,13 +429,15 @@
     copies = [pltpu.make_async_copy(ready[i], outs[i], sems.at[i]) for i in range(5)]
     for i in (0, 1, 4):
         copies[i].start()
-    rows = tiles.shape[2]
+    in_dim, hidden = gs.shape
+    tpq = tiles.shape[1] // 16
     for kind, out in ((0, gs), (1, gn)):
-        for n in range(2 * out.shape[0] // 8):
-            rt, c, part = n // 2, n % 2, (n % (rows // 8)) * 8
-            out[rt * 8 : (rt + 1) * 8, c * 128 : (c + 1) * 128] = tiles[
-                kind, n // (rows // 8), part : part + 8, :
-            ]
+        for r in range(in_dim // 16):
+            for c in range(hidden // 128):
+                n = (kind * in_dim // 16 + r) * (hidden // 128) + c
+                out[r * 16 : (r + 1) * 16, c * 128 : (c + 1) * 128] = tiles[
+                    n // tpq, (n % tpq) * 16 : (n % tpq + 1) * 16, :
+                ].astype(F32)
         copies[2 + kind].start()
     for copy in copies:
         copy.wait()
@@ -453,8 +463,7 @@
     tile_count = tile_values.shape[0]
     nb = vertices // BLOCK
     vc = vertices // y_size
-    tpq = (in_dim // 8) * (hidden // 128) // xz
-    ext = 8 * tpq + 1
+    rows = (2 * in_dim * hidden) // (128 * xz)
     dims = (
         dom_size,
         y_size,
@@ -471,7 +480,7 @@
         out_shape=(
             jax.ShapeDtypeStruct((hr, vertices), BF16),
             jax.ShapeDtypeStruct((fr, vertices), BF16),
-            jax.ShapeDtypeStruct((2, xz, 8 * tpq, 128), F32),
+            jax.ShapeDtypeStruct((xz, rows, 128), BF16),
             jax.ShapeDtypeStruct((1, hidden), F32),
         ),
         in_specs=[hbm] * 9,
@@ -508,20 +517,22 @@
             pltpu.VMEM((nb * fr, tile_count * fr), BF16),
             pltpu.VMEM((4, 4, fr, BLOCK), F32),
             pltpu.VMEM((4, 4, fr, BLOCK), F32),
-            pltpu.VMEM((xz, ext, 128), F32),
-            pltpu.VMEM((xz, ext, 128), F32),
-            pltpu.VMEM((xz, ext, 128), F32),
-            pltpu.VMEM((xz, ext, 128), F32),
-            pltpu.VMEM((xz, ext, 128), F32),
-            pltpu.VMEM((ext, 128), F32),
-            pltpu.VMEM((y_size, ext, 128), F32),
-            pltpu.VMEM((xz, 8 * tpq, 128), F32),
-            pltpu.VMEM((2, 1, 128), F32),
+            pltpu.VMEM((xz, rows, 128), BF16),
+            pltpu.VMEM((xz, rows, 128), BF16),
+            pltpu.VMEM((rows, 128), F32),
+            pltpu.VMEM((rows, 128), F32),
+            pltpu.VMEM((rows, 128), F32),
+            pltpu.VMEM((y_size, rows, 128), F32),
+            pltpu.VMEM((rows, 128), BF16),
+            pltpu.VMEM((4, 1, hidden), F32),
+            pltpu.VMEM((1, hidden), F32),
+            pltpu.VMEM((y_size, 1, hidden), F32),
+            pltpu.VMEM((xz // X_SIZE, 1, hidden), F32),
+            pltpu.VMEM((X_SIZE, 1, hidden), F32),
             pltpu.SemaphoreType.REGULAR,
             dma((10,)),
-            dma((13,)),
-            dma((12,)),
-            dma((xz // X_SIZE,)),
+            dma((15,)),
+            dma((15,)),
         ],
         compiler_params=pltpu.CompilerParams(
             collective_id=0, has_side_effects=True, vmem_limit_bytes=24 * 1024 * 1024

time: 48.5 us -> 47.1 us (0.971)
  Pallas kernels: 47.7 us -> 46.3 us
    pallas_call x1, Pallas kernels: 46.9 us -> 45.5 us  [local(): pl.pallas_call(functools.partial(kernel, dims), out_shape=(jax.ShapeDtype...]
where the time goes in v7:
time: 47.1 us; the launch traced here: 46.9 us
  Pallas kernels  46.3 us (98%)
  between operations  0.64 us (1%)
    pallas_call x1, Pallas kernels, local(): pl.pallas_call(functools.partial(kernel, dims), out_shape=(jax.ShapeDtype...  45.5 us

profile of v7, /device:TPU:1, one launch (start us, length us, event | category | flops | bytes accessed | tf_op | source)
XLA Modules:
  0.0 46.9 jit_solution(15413792535843748872)
XLA Ops:
  0.6 45.5 %graph_layer.1 = (bf16[32,2048]{1,0:T(8,128)(2,1)S(1)}, bf16[16,2048]{1,0:T(8,128)(2,1)S(1)}, bf16[32,16,128]{2,1,0:T(8,128)(2,1)S(1)}, f32[1,256]{1,0:T(1,128)S(1)}) custom-call(s32[64]{0:T(128)} %rows_in.1, s32[64]{0:T(128)} %cols_in.1, s32[1,4,64]{2,1,0:T(4,128)} %bitcast.3, bf16[16,2048]{1,0:T(8,128)(2,1)} %features.1, bf16[128,256]{1,0:T(8,128)(2,1)} %self_weight.1, ...), custom_call_target="tpu_custom_call" | custom-call | tf_op jit(solution)/shard_map/graph_layer/pallas_call | solution.py:478
  46.1 0.8 %place_outputs.1 = (bf16[32,2048]{1,0:T(8,128)(2,1)}, bf16[16,2048]{1,0:T(8,128)(2,1)}, f32[128,256]{1,0:T(8,128)}, f32[128,256]{1,0:T(8,128)}, f32[1,256]{1,0:T(1,128)}) custom-call(bf16[32,2048]{1,0:T(8,128)(2,1)S(1)} %get-tuple-element.14.refs_0_, bf16[16,2048]{1,0:T(8,128)(2,1)S(1)} %get-tuple-element.15.refs_1_, ...), custom_call_target="tpu_custom_call" | custom-call | tf_op jit(solution)/shard_map/place_outputs/pallas_call | solution.py:558

commit v8 on v7

--- a/solution.py
+++ b/solution.py
@@ -278,9 +278,6 @@
     cot = ct[...].reshape(hidden, vc).astype(F32)
     dpre = (cot * sigma * (1.0 + pre * (1.0 - sigma))).astype(BF16)
 
-    b_src[0] = dot_nt(jnp.ones((16, vc), BF16), dpre)[0:1]
-    bias_swap = remote(b_src.at[0], b_core, send_sem.at[4], recv_sem.at[4], sibling)
-    bias_swap.start()
     grads = dot_nt(xg[...].reshape(2 * in_dim, vc), dpre).astype(BF16)
     for rt in range(2 * in_dim // 16):
         for c in range(col_tiles):
@@ -294,6 +291,9 @@
             part.at[p], rs_recv.at[q], send_sem.at[6], recv_sem.at[6], (p * CORES + core, fy)
         ).start()
     rs_recv[q] = part[q]
+    b_src[0] = dot_nt(jnp.ones((16, vc), BF16), dpre)[0:1]
+    bias_swap = remote(b_src.at[0], b_core, send_sem.at[4], recv_sem.at[4], sibling)
+    bias_swap.start()
 
     bk[:, 0:fr] = dot_nn(w_self[...], dpre).astype(BF16).reshape(y_size, fr, vc)
     bk[:, fr : 2 * fr] = dot_nn(w_neigh[...], dpre).astype(BF16).reshape(y_size, fr, vc)
@@ -316,6 +316,13 @@
     t_src[...] = total
     swap = remote(t_src, t_core, send_sem.at[12], recv_sem.at[12], sibling)
     swap.start()
+    swap.wait_recv()
+    total = total + t_core[...]
+    y_src[...] = total
+    y_recv[fy] = total
+    for p in y_peers:
+        remote(y_src, y_recv.at[fy], send_sem.at[8], recv_sem.at[8], (dom, p)).start()
+
     drain(b_y.at[0:others], recv_sem.at[10])
     b_sum = b_y[0]
     for n in range(1, y_size):
@@ -324,18 +331,6 @@
     b_z[my_z] = b_sum
     for device in z_peers:
         remote(b_src.at[2], b_z.at[my_z], send_sem.at[11], recv_sem.at[11], device).start()
-    swap.wait_recv()
-    total = total + t_core[...]
-    y_src[...] = total
-    y_recv[fy] = total
-    for p in y_peers:
-        remote(y_src, y_recv.at[fy], send_sem.at[8], recv_sem.at[8], (dom, p)).start()
-    for p in y_peers:
-        remote(
-            act.at[p], columns(activated, fy), send_sem.at[9], recv_sem.at[9], (dom, p)
-        ).start()
-    own_act = pltpu.make_async_copy(act.at[fy], columns(activated, fy), local_sem.at[9])
-    own_act.start()
 
     drain(bkr.at[0:others], recv_sem.at[5])
     for b in range(nb):
@@ -366,6 +361,12 @@
         remote(
             g_src, grad_tiles.at[q], send_sem.at[13], recv_sem.at[13], (p * CORES + core, fy)
         ).start()
+    for p in y_peers:
+        remote(
+            act.at[p], columns(activated, fy), send_sem.at[9], recv_sem.at[9], (dom, p)
+        ).start()
+    own_act = pltpu.make_async_copy(act.at[fy], columns(activated, fy), local_sem.at[9])
+    own_act.start()
     stores = [pltpu.make_async_copy(g_src, grad_tiles.at[q], local_sem.at[2])]
     drain(b_z.at[0 : z_size - 1], recv_sem.at[11])
     b_sum = b_z[0]
@@ -399,9 +400,6 @@
     gb[...] = b_sum * norm_scale
     stores.append(pltpu.make_async_copy(gb, grad_bias, local_sem.at[1]))
     stores[-1].start()
-    own_act.wait()
-    drain(activated.at[:, 0 : others * vc], recv_sem.at[9])
-    drain(grad_tiles.at[0 : xz - 1], recv_sem.at[13])
 
     drain(stage, send_sem.at[0])
     drain(xg.at[0, 0:others], send_sem.at[1])
@@ -412,12 +410,15 @@
     drain(rs_recv.at[0 : xz - 1], send_sem.at[6])
     drain(rb_recv, send_sem.at[7])
     drain(y_recv.at[0:others], send_sem.at[8])
-    drain(activated.at[:, 0 : others * vc], send_sem.at[9])
     drain(b_y.at[0:others], send_sem.at[10])
     drain(b_z.at[0 : z_size - 1], send_sem.at[11])
     swap.wait_send()
+    own_act.wait()
+    drain(b_x.at[0 : X_SIZE - 1], send_sem.at[14])
+    drain(activated.at[:, 0 : others * vc], send_sem.at[9])
     drain(rs_recv.at[0 : xz - 1], send_sem.at[13])
-    drain(b_x.at[0 : X_SIZE - 1], send_sem.at[14])
+    drain(grad_tiles.at[0 : xz - 1], recv_sem.at[13])
+    drain(activated.at[:, 0 : others * vc], recv_sem.at[9])
     for copy in stores:
         copy.wait()
 

time: 47.1 us -> 46.5 us (0.987)
  Pallas kernels: 46.3 us -> 45.8 us
    pallas_call x1, Pallas kernels: 45.5 us -> 45 us  [local(): pl.pallas_call(functools.partial(kernel, dims), out_shape=(jax.ShapeDtype...]
where the time goes in v8:
time: 46.5 us; the launch traced here: 46.4 us
  Pallas kernels  45.8 us (98%)
  between operations  0.64 us (1%)
    pallas_call x1, Pallas kernels, local(): pl.pallas_call(functools.partial(kernel, dims), out_shape=(jax.ShapeDtype...  45 us

profile of v8, /device:TPU:1, one launch (start us, length us, event | category | flops | bytes accessed | tf_op | source)
XLA Modules:
  0.0 46.4 jit_solution(13619285853937026205)
XLA Ops:
  0.6 45.0 %graph_layer.1 = (bf16[32,2048]{1,0:T(8,128)(2,1)S(1)}, bf16[16,2048]{1,0:T(8,128)(2,1)S(1)}, bf16[32,16,128]{2,1,0:T(8,128)(2,1)S(1)}, f32[1,256]{1,0:T(1,128)S(1)}) custom-call(s32[64]{0:T(128)} %rows_in.1, s32[64]{0:T(128)} %cols_in.1, s32[1,4,64]{2,1,0:T(4,128)} %bitcast.3, bf16[16,2048]{1,0:T(8,128)(2,1)} %features.1, bf16[128,256]{1,0:T(8,128)(2,1)} %self_weight.1, ...), custom_call_target="tpu_custom_call" | custom-call | tf_op jit(solution)/shard_map/graph_layer/pallas_call | solution.py:479
  45.6 0.8 %place_outputs.1 = (bf16[32,2048]{1,0:T(8,128)(2,1)}, bf16[16,2048]{1,0:T(8,128)(2,1)}, f32[128,256]{1,0:T(8,128)}, f32[128,256]{1,0:T(8,128)}, f32[1,256]{1,0:T(1,128)}) custom-call(bf16[32,2048]{1,0:T(8,128)(2,1)S(1)} %get-tuple-element.14.refs_0_, bf16[16,2048]{1,0:T(8,128)(2,1)S(1)} %get-tuple-element.15.refs_1_, ...), custom_call_target="tpu_custom_call" | custom-call | tf_op jit(solution)/shard_map/place_outputs/pallas_call | solution.py:559

commit v9 on v8

--- a/solution.py
+++ b/solution.py
@@ -181,7 +181,8 @@
         ((lax.rem(my_z + d, z_size) * X_SIZE + my_x) * CORES + core, fy)
         for d in sorted(range(1, z_size), key=lambda d: -ring(d, z_size))
     ]
-    greet = z_peers + [(dom, p) for p in y_peers]
+    greet = [device for pair in zip(z_peers, [(dom, p) for p in y_peers]) for device in pair]
+    greet += z_peers[y_size - 1 :] + [(dom, p) for p in y_peers[z_size - 1 :]]
     for off in (1, dom_size - 1, 2, dom_size - 2):
         greet.append((lax.rem(dom + off, dom_size), fy))
     x_peers = [

time: 46.5 us -> 46.6 us (level)
  no operation moved by 1% of the time
where the time goes in v9:
time: 46.6 us; the launch traced here: 46.4 us
  Pallas kernels  45.8 us (98%)
  between operations  0.64 us (1%)
    pallas_call x1, Pallas kernels, local(): pl.pallas_call(functools.partial(kernel, dims), out_shape=(jax.ShapeDtype...  45 us

profile of v9, /device:TPU:1, one launch (start us, length us, event | category | flops | bytes accessed | tf_op | source)
XLA Modules:
  0.0 46.4 jit_solution(11835012899278740510)
XLA Ops:
  0.6 45.0 %graph_layer.1 = (bf16[32,2048]{1,0:T(8,128)(2,1)S(1)}, bf16[16,2048]{1,0:T(8,128)(2,1)S(1)}, bf16[32,16,128]{2,1,0:T(8,128)(2,1)S(1)}, f32[1,256]{1,0:T(1,128)S(1)}) custom-call(s32[64]{0:T(128)} %rows_in.1, s32[64]{0:T(128)} %cols_in.1, s32[1,4,64]{2,1,0:T(4,128)} %bitcast.3, bf16[16,2048]{1,0:T(8,128)(2,1)} %features.1, bf16[128,256]{1,0:T(8,128)(2,1)} %self_weight.1, ...), custom_call_target="tpu_custom_call" | custom-call | tf_op jit(solution)/shard_map/graph_layer/pallas_call | solution.py:480
  45.6 0.8 %place_outputs.1 = (bf16[32,2048]{1,0:T(8,128)(2,1)}, bf16[16,2048]{1,0:T(8,128)(2,1)}, f32[128,256]{1,0:T(8,128)}, f32[128,256]{1,0:T(8,128)}, f32[1,256]{1,0:T(1,128)}) custom-call(bf16[32,2048]{1,0:T(8,128)(2,1)S(1)} %get-tuple-element.14.refs_0_, bf16[16,2048]{1,0:T(8,128)(2,1)S(1)} %get-tuple-element.15.refs_1_, ...), custom_call_target="tpu_custom_call" | custom-call | tf_op jit(solution)/shard_map/place_outputs/pallas_call | solution.py:560
